TPU v7x, 32 devices: a whole 2x2x4 slice. The times are simulated.
32 devices in a mesh: cfg: 2 (over core), req: 4 (over y, x), tp: 4 (over z).
Axes of the slice: x: 2, y: 2, z: 4, core: 2. Of those that a mesh axis runs over, the one named last changes fastest.
Arguments:
- latent: float32 [1536, 64], P(('req', 'tp')), may hold values from -6 to 6
- states: float32 [2, 1536, 1536], P('cfg', ('req', 'tp')), may hold values from -12 to 12
- token_counts: int32 [3], replicated, may hold values from 1 to 960, 1536 in all
- text_lens: int32 [2, 3], P('cfg'), may hold values from 1 to 512, 768 in all within a row
- steps_index: int32 [3], replicated, may hold values from 0 to 49
- modulation: float32 [3, 6, 1536], replicated, may hold values from -3 to 3
- self_qkv: bfloat16 [1536, 3, 1536], P(None, None, 'tp'), may hold values from -0.15625 to 0.15625
- self_out: bfloat16 [1536, 1536], P('tp'), may hold values from -0.15625 to 0.15625
- qk_gains: float32 [4, 1536], P(None, 'tp'), may hold values from 0.8 to 2
- cross_query: bfloat16 [1536, 1536], P(None, 'tp'), may hold values from -1 to 1
- cross_out: bfloat16 [1536, 1536], P('tp'), may hold values from -0.15625 to 0.15625
- cross_gain: float32 [1536], replicated, may hold values from 0.25 to 1.75
- text_kv: bfloat16 [2, 3, 2, 512, 1536], P('cfg', None, None, None, 'tp'), may hold values from -6 to 6
- ffn_in_weight: bfloat16 [8960, 1536], P(('cfg', 'tp')), may hold values from -0.15625 to 0.15625
- ffn_out_weight: bfloat16 [8960, 1536], P(('cfg', 'tp')), may hold values from -0.0625 to 0.0625
- head_weight: bfloat16 [1536, 64], replicated, may hold values from -0.15625 to 0.15625
Outputs:
- new_latent: float32 [1536, 64], P(('req', 'tp'), 'cfg')
- velocity: float32 [1536, 64], P(('req', 'tp'), 'cfg')
- peak: float32 [3], replicated
Inputs may be any that keep to these rules, and one draw needn't show every extreme that they name: `token_counts`: the counts sum to 1536 and the largest is exactly 960. `text_lens`: in each prompt half the counts sum to 768 and the largest is exactly 512.
All inputs are finite; a program needn't handle non-finite values.
Results may differ from a plain program's by a relative error of at most 0.03.
Values may be sent and summed in bfloat16 or wider, within the bound.
A program may use at most 64 MiB of HBM per device.

v0:
```python
import jax
import jax.numpy as jnp
from jax import lax
from jax.sharding import PartitionSpec as P

HEADS = 12
HD = 128
STEPS = 50


key_block = 1024
guide_scale = 5.0
rescale_mix = 0.7
flow_shift = 5.0
norm_eps = 1e-06
stat_eps = 1e-05


def swapped(value, axis, stride):
    mask = 2**stride
    pairs = [(source, source ^ mask) for source in range(lax.axis_size(axis))]
    return lax.ppermute(value, axis, pairs)


def layer_norm(values):
    average = jnp.mean(values, axis=-1, keepdims=True)
    centered = values - average
    spread = jnp.mean(centered * centered, axis=-1, keepdims=True)
    return centered * lax.rsqrt(spread + norm_eps)


def rms_scale(values, square_sum, width, gains):
    return (values * lax.rsqrt(square_sum / width + norm_eps)[:, None] * gains).astype(jnp.bfloat16)


def request_of(positions, request_ends):
    return jnp.sum((positions[:, None] >= request_ends[None, :]).astype(jnp.int32), axis=1)


def presence(request_ids, request_count):
    return jnp.any(
        request_ids[:, None] == jnp.arange(request_count, dtype=jnp.int32)[None, :], axis=0
    )


def attend(running, queries, query_req, key_rows, value_rows, key_req, head_count, head_width):
    numerator, denominator = running
    query_count = queries.shape[0]
    key_count = key_rows.shape[0]
    scores = jnp.einsum(
        "qhd,khd->hqk",
        queries.reshape(query_count, head_count, head_width),
        key_rows.reshape(key_count, head_count, head_width),
        preferred_element_type=jnp.float32,
    ) * head_width ** (-0.5)
    same_req = query_req[:, None] == key_req[None, :]
    weights = jnp.where(same_req[None, :, :], jnp.exp(scores), 0.0)
    partial_sum = jnp.einsum(
        "hqk,khd->qhd",
        weights.astype(jnp.bfloat16),
        value_rows.reshape(key_count, head_count, head_width),
        preferred_element_type=jnp.float32,
    )
    return (
        numerator + partial_sum.reshape(query_count, head_count * head_width),
        denominator + jnp.transpose(jnp.sum(weights, axis=2)),
    )


def finish_heads(running, keep_cols, head_count, head_width):
    numerator, denominator = running
    query_count = numerator.shape[0]
    mixed = numerator.reshape(query_count, head_count, head_width) / denominator[:, :, None]
    return (mixed.reshape(query_count, head_count * head_width) * keep_cols).astype(jnp.bfloat16)


def fold_keys(
    running,
    queries,
    query_req,
    key_rows,
    value_rows,
    first_row,
    request_ends,
    all_tokens,
    head_count,
    head_width,
):
    key_total = key_rows.shape[0]
    request_count = request_ends.shape[0]
    wanted = presence(query_req, request_count)

    def visit_block(current, key_part, value_part, part_start):
        part_rows = key_part.shape[0]
        key_pos = part_start + jnp.arange(part_rows, dtype=jnp.int32)
        inside = (key_pos >= 0) & (key_pos < all_tokens)
        key_req = jnp.where(inside, request_of(key_pos, request_ends), -1)
        intersection = jnp.any(wanted & presence(key_req, request_count))

        def compute(state_now):
            return attend(
                state_now, queries, query_req, key_part, value_part, key_req, head_count, head_width
            )

        def skip(state_now):
            return state_now

        return lax.cond(intersection, compute, skip, current)

    full_blocks = key_total // key_block
    key_full = key_rows[: full_blocks * key_block].reshape(
        full_blocks, key_block, key_rows.shape[1]
    )
    value_full = value_rows[: full_blocks * key_block].reshape(
        full_blocks, key_block, value_rows.shape[1]
    )
    block_starts = key_block * jnp.arange(full_blocks, dtype=jnp.int32)

    def scan_step(current, block_inputs):
        return (visit_block(current, block_inputs[0], block_inputs[1], block_inputs[2]), None)

    running, unused = lax.scan(scan_step, running, (key_full, value_full, block_starts))
    if key_total > full_blocks * key_block:
        running = visit_block(
            running,
            key_rows[full_blocks * key_block :],
            value_rows[full_blocks * key_block :],
            first_row + full_blocks * key_block,
        )
    return running


def gather_project(row_block, weight):
    return jnp.dot(
        lax.all_gather(row_block, "tp", axis=0, tiled=True),
        weight,
        preferred_element_type=jnp.float32,
    )


def scatter_project(mixed, weight):
    return lax.psum_scatter(
        jnp.dot(mixed, weight, preferred_element_type=jnp.float32).astype(jnp.bfloat16),
        "tp",
        scatter_dimension=0,
        tiled=True,
    ).astype(jnp.float32)


def feed_forward(ffn_rows, in_weight, out_weight):
    up_part = lax.dot_general(
        lax.all_gather(ffn_rows, ("cfg", "tp"), axis=0, tiled=True),
        in_weight,
        (((1,), (1,)), ((), ())),
        preferred_element_type=jnp.float32,
    )
    activated = jax.nn.gelu(up_part, approximate=True).astype(jnp.bfloat16)
    return lax.psum_scatter(
        jnp.dot(activated, out_weight, preferred_element_type=jnp.float32).astype(jnp.bfloat16),
        ("cfg", "tp"),
        scatter_dimension=0,
        tiled=True,
    ).astype(jnp.float32)


def noise_level(step_value):
    fraction = 1.0 - step_value / STEPS
    return flow_shift * fraction / (1.0 + (flow_shift - 1.0) * fraction)


def shards(
    latent,
    states,
    token_counts,
    text_lens,
    steps_index,
    modulation,
    self_qkv,
    self_out,
    qk_gains,
    cross_query,
    cross_out,
    cross_gain,
    text_kv,
    ffn_in_weight,
    ffn_out_weight,
    head_weight,
):
    row_count = latent.shape[0]
    head_width = HD
    local_cols = self_out.shape[0]
    head_count = local_cols // head_width
    model_width = head_weight.shape[0]
    request_count = token_counts.shape[0]
    tp_parts = lax.axis_size("tp")
    block_rows = row_count * tp_parts
    all_tokens = block_rows * lax.axis_size("req")
    request_ends = jnp.cumsum(token_counts)
    request_range = jnp.arange(request_count, dtype=jnp.int32)
    row_pos = (lax.axis_index("req") * tp_parts + lax.axis_index("tp")) * row_count + jnp.arange(
        row_count, dtype=jnp.int32
    )
    row_onehot = (request_of(row_pos, request_ends)[:, None] == request_range[None, :]).astype(
        jnp.float32
    )
    block_first = lax.axis_index("req") * block_rows
    query_req = request_of(block_first + jnp.arange(block_rows, dtype=jnp.int32), request_ends)
    head_ids = lax.axis_index("tp") * head_count + jnp.arange(head_count, dtype=jnp.int32)
    keep_cols = jnp.repeat((head_ids < HEADS).astype(jnp.float32), head_width)
    hidden_zero = states[0]
    row_mods = jnp.dot(
        row_onehot,
        modulation.reshape(request_count, 6 * model_width),
        precision=lax.Precision.HIGHEST,
    )
    shift_attn = row_mods[:, :model_width]
    scale_attn = row_mods[:, model_width : 2 * model_width]
    gate_attn = row_mods[:, 2 * model_width : 3 * model_width]
    shift_ffn = row_mods[:, 3 * model_width : 4 * model_width]
    scale_ffn = row_mods[:, 4 * model_width : 5 * model_width]
    gate_ffn = row_mods[:, 5 * model_width :]
    normed = (layer_norm(hidden_zero) * (1.0 + scale_attn) + shift_attn).astype(jnp.bfloat16)
    projected = gather_project(normed, self_qkv.reshape(model_width, 3 * local_cols))
    query_raw = projected[:, :local_cols] * keep_cols
    key_raw = projected[:, local_cols : 2 * local_cols] * keep_cols
    query_sq, key_sq = lax.psum(
        (jnp.sum(query_raw * query_raw, axis=1), jnp.sum(key_raw * key_raw, axis=1)), "tp"
    )
    queries = rms_scale(query_raw, query_sq, model_width, qk_gains[0])
    key_rows = rms_scale(key_raw, key_sq, model_width, qk_gains[1])
    value_rows = projected[:, 2 * local_cols :].astype(jnp.bfloat16)
    start_state = (
        jnp.zeros((block_rows, local_cols), jnp.float32),
        jnp.zeros((block_rows, head_count), jnp.float32),
    )
    running = fold_keys(
        start_state,
        queries,
        query_req,
        lax.all_gather(key_rows, "req", axis=0, tiled=True),
        lax.all_gather(value_rows, "req", axis=0, tiled=True),
        jnp.int32(0),
        request_ends,
        all_tokens,
        head_count,
        head_width,
    )
    self_mix = finish_heads(running, keep_cols, head_count, head_width)
    hidden_one = hidden_zero + gate_attn * scatter_project(self_mix, self_out)
    cross_in = (layer_norm(hidden_one) * cross_gain).astype(jnp.bfloat16)
    cross_raw = gather_project(cross_in, cross_query) * keep_cols
    text_local = text_kv[0]
    text_slots = text_local.shape[2]
    text_raw = (
        text_local[:, 0].reshape(request_count * text_slots, local_cols).astype(jnp.float32)
        * keep_cols
    )
    cross_sq, text_sq = lax.psum(
        (jnp.sum(cross_raw * cross_raw, axis=1), jnp.sum(text_raw * text_raw, axis=1)), "tp"
    )
    cross_q = rms_scale(cross_raw, cross_sq, model_width, qk_gains[2])
    text_keys = rms_scale(text_raw, text_sq, model_width, qk_gains[3])
    text_values = text_local[:, 1].reshape(request_count * text_slots, local_cols)
    text_req = jnp.repeat(request_range, text_slots)
    text_pos = jnp.tile(jnp.arange(text_slots, dtype=jnp.int32), request_count)
    text_limit = jnp.sum(
        jnp.where(text_req[:, None] == request_range[None, :], text_lens[0][None, :], 0), axis=1
    )
    text_req = jnp.where(text_pos < text_limit, text_req, -1)
    cross_state = attend(
        start_state, cross_q, query_req, text_keys, text_values, text_req, head_count, head_width
    )
    cross_mix = finish_heads(cross_state, keep_cols, head_count, head_width)
    hidden_two = hidden_one + scatter_project(cross_mix, cross_out)
    ffn_in = (layer_norm(hidden_two) * (1.0 + scale_ffn) + shift_ffn).astype(jnp.bfloat16)
    hidden_three = hidden_two + gate_ffn * feed_forward(ffn_in, ffn_in_weight, ffn_out_weight)
    velocity_own = jnp.dot(
        layer_norm(hidden_three).astype(jnp.bfloat16),
        head_weight,
        preferred_element_type=jnp.float32,
    )
    velocity_other = swapped(velocity_own, "cfg", 0)
    first_half = lax.axis_index("cfg") == 0
    cond_speed = jnp.where(first_half, velocity_own, velocity_other)
    plain_speed = jnp.where(first_half, velocity_other, velocity_own)
    guided = plain_speed + guide_scale * (cond_speed - plain_speed)
    row_squares = jnp.stack(
        [jnp.sum(cond_speed * cond_speed, axis=1), jnp.sum(guided * guided, axis=1)], axis=1
    )
    square_sums = jnp.dot(jnp.transpose(row_onehot), row_squares, precision=lax.Precision.HIGHEST)
    peak_speed = jnp.max(row_onehot * jnp.max(jnp.abs(guided), axis=1)[:, None], axis=0)
    square_sums = lax.psum(square_sums, ("req", "tp"))
    peak_speed = lax.pmax(peak_speed, ("req", "tp"))
    entry_counts = token_counts.astype(jnp.float32) * guided.shape[1]
    cond_rms = jnp.sqrt(square_sums[:, 0] / entry_counts + stat_eps)
    guided_rms = jnp.sqrt(square_sums[:, 1] / entry_counts + stat_eps)
    factor = rescale_mix * cond_rms / guided_rms + (1.0 - rescale_mix)
    step_value = steps_index.astype(jnp.float32)
    delta_t = noise_level(step_value + 1.0) - noise_level(step_value)
    per_row = jnp.dot(
        row_onehot, jnp.stack([factor, delta_t], axis=1), precision=lax.Precision.HIGHEST
    )
    velocity = per_row[:, 0:1] * guided
    new_latent = latent + per_row[:, 1:2] * velocity
    own_cols = guided.shape[1] // lax.axis_size("cfg")
    col_start = lax.axis_index("cfg") * own_cols
    velocity_part = lax.dynamic_slice_in_dim(velocity, col_start, own_cols, 1)
    latent_part = lax.dynamic_slice_in_dim(new_latent, col_start, own_cols, 1)
    return (latent_part, velocity_part, factor * peak_speed)


def solution(mesh):
    in_specs = (
        P(("req", "tp"), None),
        P("cfg", ("req", "tp"), None),
        P(),
        P("cfg", None),
        P(),
        P(),
        P(None, None, "tp"),
        P("tp", None),
        P(None, "tp"),
        P(None, "tp"),
        P("tp", None),
        P(),
        P("cfg", None, None, None, "tp"),
        P(("cfg", "tp"), None),
        P(("cfg", "tp"), None),
        P(),
    )
    out_specs = (P(("req", "tp"), "cfg"), P(("req", "tp"), "cfg"), P())
    return jax.shard_map(shards, mesh=mesh, in_specs=in_specs, out_specs=out_specs, check_vma=False)
```

profile of v0, /device:TPU:0, one launch (start us, length us, event | category | flops | bytes accessed | tf_op | source)
XLA Modules:
  0.0 494.0 jit_solution(634086430429006287)
XLA Ops:
  12.5 2.6 fusion.67
  17.8 6.1 %copy.54 = bf16[1536,3,384]{0,2,1:T(8,128)(2,1)} copy(bf16[1536,3,384]{2,0,1:T(8,128)(2,1)} %param.26) | data formatting | bytes 7077888 | tf_op args[6]
  24.0 27.0 %all-gather.6.cloned.1.call-done = bf16[384,1536]{1,0:T(8,128)(2,1)} async-done(((bf16[96,1536]{1,0:T(8,128)(2,1)}), bf16[384,1536]{1,0:T(8,128)(2,1)}) %all-gather.6.cloned.1.call-update) | async-done | bytes 1179664 | tf_op jit(solution)/shard_map/all_gather | solution.py:135
  51.1 4.1 fusion.88
  56.6 9.9 %all-reduce.1 = (f32[384]{0:T(512)S(1)}, f32[384]{0:T(512)S(1)}) all-reduce(f32[384]{0:T(512)S(1)} %get-tuple-element.153, f32[384]{0:T(512)S(1)} %get-tuple-element.152), channel_id=1, replica_groups=mesh['cfg'=2,'req'=4,'tp'=4] {'tp'}, use_global_device_ids=true, to_apply=%region_13.14 | all-reduce | flops 768 | bytes 6144 | tf_op jit(solution)/shard_map/psum | solution.py:226
  66.5 2.3 multiply_convert_fusion.6
  74.2 20.6 %all-gather.8.cloned.1.call-done = bf16[1536,384]{1,0:T(8,128)(2,1)} async-done(((bf16[384,384]{1,0:T(8,128)(2,1)}), bf16[1536,384]{1,0:T(8,128)(2,1)}) %all-gather.8.cloned.1.call-update) | async-done | bytes 1179664 | tf_op jit(solution)/shard_map/all_gather | solution.py:240
  94.8 2.1 slice.100
  96.9 27.5 %all-gather.10.cloned.1.call-done = bf16[1536,384]{1,0:T(8,128)(2,1)} async-done(((bf16[384,384]{1,0:T(8,128)(2,1)}), bf16[1536,384]{1,0:T(8,128)(2,1)}) %all-gather.10.cloned.1.call-update) | async-done | bytes 1179664 | tf_op jit(solution)/shard_map/all_gather | solution.py:241
  124.4 2.1 slice.102
  126.4 18.0 %conditional.2 = ((f32[384,384]{0,1:T(8,128)}, f32[384,3]{0,1:T(4,128)S(1)})) conditional(s32[]{:T(128)} %convert_element_type.107, (f32[384,384]{0,1:T(8,128)}, f32[384,3]{0,1:T(4,128)S(1)}) %tuple.23, (s32[384]{0:T(512)S(1)}, s32[1024]{0:T(1024)S(1)}, bf16[384,384]{1,0:T(8,128)(2,1)}, bf16[1024,384]{1,0:T(8,128)(2,1)}, ...), branch_computations={%region_16.17_spmd, %region_17.19_spmd} | conditional | flops 611598336 | bytes 18603544 | solution.py:108
  127.5 2.3 copy.56
  129.8 1.8 copy.55
  131.6 4.8 fusion
  136.4 2.3 copy.57
  138.8 3.7 fusion.2
  142.5 2.0 bitcast_add_fusion
  144.4 19.9 %conditional.3 = (f32[384,3]{0,1:T(4,128)S(1)}, f32[384,384]{1,0:T(8,128)}) conditional(s32[]{:T(128)} %convert_element_type.105, (f32[384,384]{0,1:T(8,128)}, f32[384,3]{0,1:T(4,128)S(1)}) %get-tuple-element.200, (s32[384]{0:T(512)S(1)}, s32[512]{0:T(512)S(1)}, s32[512]{0:T(512)S(1)}, bf16[384,384]{1,0:T(8,128)(2,1)}, ...), branch_computations={%region_19.20_spmd, %region_20.22_spmd} | conditional | flops 305874944 | bytes 16838160 | solution.py:108
  145.3 2.5 copy.59
  149.5 1.8 copy.58
  151.4 3.2 fusion.9
  154.6 2.4 copy.60
  158.0 2.3 fusion.11
  160.3 1.9 bitcast_add_fusion.2
  162.2 2.1 copy.76
  165.2 2.1 copy.62
  167.3 3.4 convolution_convert_fusion.2
  171.0 29.1 %reduce-scatter.4.cloned.1.call-done = bf16[96,1536]{1,0:T(8,128)(2,1)} async-done(((bf16[384,1536]{1,0:T(8,128)(2,1)}), bf16[96,1536]{1,0:T(8,128)(2,1)}) %reduce-scatter.4.cloned.1.call-update) | async-done | bytes 294928 | tf_op jit(solution)/shard_map/reduce_scatter | solution.py:142
  205.1 3.7 slice_convert_fusion
  208.9 4.6 reshape.287
  213.5 4.1 reshape_reshape_squeeze.3
  218.9 13.8 %all-gather.12.cloned.1.call-done = bf16[384,1536]{1,0:T(8,128)(2,1)} async-done(((bf16[96,1536]{1,0:T(8,128)(2,1)}), bf16[384,1536]{1,0:T(8,128)(2,1)}) %all-gather.12.cloned.1.call-update) | async-done | bytes 1179664 | tf_op jit(solution)/shard_map/all_gather | solution.py:135
  232.7 3.2 multiply_reduce_fusion.3
  236.0 16.9 %all-reduce = (f32[384]{0:T(512)S(1)}, f32[1536]{0:T(1024)S(1)}) all-reduce(f32[384]{0:T(512)S(1)} %get-tuple-element.186, f32[1536]{0:T(1024)S(1)} %reduce_sum.214), channel_id=1, replica_groups=mesh['cfg'=2,'req'=4,'tp'=4] {'tp'}, use_global_device_ids=true, to_apply=%region_27.28 | all-reduce | flops 1920 | bytes 15360 | tf_op jit(solution)/shard_map/psum | solution.py:258
  252.8 2.0 multiply_convert_fusion.3
  254.8 1.8 copy.64
  256.7 5.6 %multiply_convert_fusion = bf16[1536,3,128]{2,1,0:T(4,128)(2,1)S(1)} fusion(f32[1536,3,128]{2,1,0:T(4,128)} %reshape.287, f32[3,128]{1,0:T(4,128)S(1)} %bitcast.99, f32[1536]{0:T(1024)S(1)} %add_rsqrt_fusion, f32[3]{0:T(128)S(1)} %compare_convert_fusion), kind=kLoop, calls=%fused_computation.42 | loop fusion | flops 2359296 | bytes 3546636 | tf_op jit(solution)/shard_map/convert_element_type | solution.py:33
  262.3 2.7 fusion.18
  265.1 2.3 fusion.44
  267.4 2.1 copy.68
  269.6 3.2 convolution_convert_fusion.1
  272.9 27.4 %reduce-scatter.6.cloned.1.call-done = bf16[96,1536]{1,0:T(8,128)(2,1)} async-done(((bf16[384,1536]{1,0:T(8,128)(2,1)}), bf16[96,1536]{1,0:T(8,128)(2,1)}) %reduce-scatter.6.cloned.1.call-update) | async-done | bytes 294928 | tf_op jit(solution)/shard_map/reduce_scatter | solution.py:142
  303.0 2.4 fusion.49
  305.7 30.2 %all-gather.14.cloned.1.call-done = bf16[768,1536]{1,0:T(8,128)(2,1)} async-done(((bf16[96,1536]{1,0:T(8,128)(2,1)}), bf16[768,1536]{1,0:T(8,128)(2,1)}) %all-gather.14.cloned.1.call-update) | async-done | bytes 2359312 | tf_op jit(solution)/shard_map/all_gather | solution.py:152
  335.9 15.4 %convolution_convert_fusion = bf16[768,1536]{1,0:T(8,128)(2,1)} fusion(bf16[1120,1536]{1,0:T(8,128)(2,1)S(1)} %copy-done, bf16[768,1536]{1,0:T(8,128)(2,1)} %all-gather.14.cloned.1.call-done, bf16[1120,1536]{1,0:T(8,128)(2,1)} %param.33), kind=kOutput, calls=%fused_computation.41 | convolution fusion | flops 5293744128 | bytes 11599872 | tf_op jit(solution)/shard_map/dot_general | solution.py:159
  351.4 53.3 %reduce-scatter.8.cloned.1.call-done = bf16[96,1536]{1,0:T(8,128)(2,1)} async-done(((bf16[768,1536]{1,0:T(8,128)(2,1)}), bf16[96,1536]{1,0:T(8,128)(2,1)}) %reduce-scatter.8.cloned.1.call-update) | async-done | bytes 294928 | tf_op jit(solution)/shard_map/reduce_scatter | solution.py:158
  408.4 39.9 %psum.39 = f32[3,2]{0,1:T(2,128)S(1)} all-reduce(f32[3,2]{0,1:T(2,128)S(1)} %fusion.66), channel_id=1, replica_groups=mesh['cfg'=2,'req'=4,'tp'=4] {'req','tp'}, use_global_device_ids=true, to_apply=%region_39.40 | all-reduce | flops 6 | bytes 48 | tf_op jit(solution)/shard_map/psum | solution.py:292
  448.3 36.8 %pmax.7 = f32[3]{0:T(128)S(1)} all-reduce(f32[3]{0:T(128)S(1)} %select_reduce_fusion.1), channel_id=1, replica_groups=mesh['cfg'=2,'req'=4,'tp'=4] {'req','tp'}, use_global_device_ids=true, to_apply=%region_42.43 | all-reduce | flops 3 | bytes 24 | tf_op jit(solution)/shard_map/pmax | solution.py:293
  (116 shorter events, 34.6 us)
Async XLA Ops:
  7.2 328.8 %copy-start = (bf16[1120,1536]{1,0:T(8,128)(2,1)S(1)}, bf16[1120,1536]{1,0:T(8,128)(2,1)}, u32[]{:S(2)}) copy-start(bf16[1120,1536]{1,0:T(8,128)(2,1)} %param.34) | copy-start | bytes 10321924
  7.2 43.9 %all-gather.6.cloned.1.call-start = ((), (), s32[]{:S(2)}) async-start(), calls=%async_computation.3 | async-start | bytes 1474560 | tf_op jit(solution)/shard_map/all_gather | solution.py:135
  12.4 4.4 copy-start.3
  15.0 1.8 copy-start.2
  17.8 6.1 %copy-start.10 = (f32[4,384]{1,0:T(4,128)S(1)}, f32[4,384]{1,0:T(4,128)}, u32[]{:S(2)}) copy-start(f32[4,384]{1,0:T(4,128)} %param.28) | copy-start | bytes 18436
  17.8 77.0 %all-gather.8.cloned.1.call-start = ((), (), s32[]{:S(2)}) async-start(), calls=%async_computation.4 | async-start | bytes 1474560 | tf_op jit(solution)/shard_map/all_gather | solution.py:240
  55.2 1.2 copy-start.4
  68.7 55.6 %all-gather.10.cloned.1.call-start = ((), (), s32[]{:S(2)}) async-start(), calls=%async_computation.5 | async-start | bytes 1474560 | tf_op jit(solution)/shard_map/all_gather | solution.py:241
  70.6 129.5 %reduce-scatter.4.cloned.1.call-start = ((), (), s32[]{:S(2)}) async-start(), calls=%async_computation.6 | async-start | bytes 1474560 | tf_op jit(solution)/shard_map/reduce_scatter | solution.py:142
  170.8 31.8 %copy-start.9 = (f32[1536]{0:T(1024)S(1)}, f32[1536]{0:T(1024)}, u32[]{:S(2)}) copy-start(f32[1536]{0:T(1024)} %param.31) | copy-start | bytes 18436
  170.8 61.9 %all-gather.12.cloned.1.call-start = ((), (), s32[]{:S(2)}) async-start(), calls=%async_computation.7 | async-start | bytes 1474560 | tf_op jit(solution)/shard_map/all_gather | solution.py:135
  201.6 0.9 copy-start.1
  203.4 96.9 %reduce-scatter.6.cloned.1.call-start = ((), (), s32[]{:S(2)}) async-start(), calls=%async_computation.8 | async-start | bytes 1474560 | tf_op jit(solution)/shard_map/reduce_scatter | solution.py:142
  213.4 4.1 copy-start.11
  256.6 5.6 %copy-start.6 = (pred[384,1536]{1,0:T(8,128)(4,1)S(1)}, pred[384,1536]{1,0:T(8,128)(4,1)}, u32[]{:S(2)}) copy-start(pred[384,1536]{1,0:T(8,128)(4,1)} %broadcast_compare_fusion.2) | copy-start | bytes 1769476
  256.7 5.6 %copy-start.7 = (bf16[384,384]{0,1:T(8,128)(2,1)S(1)}, bf16[384,384]{0,1:T(8,128)(2,1)}, u32[]{:S(2)}) copy-start(bf16[384,384]{0,1:T(8,128)(2,1)} %copy.64) | copy-start | bytes 884740
  262.3 2.7 copy-start.5
  272.8 63.1 %all-gather.14.cloned.1.call-start = ((), (), s32[]{:S(2)}) async-start(), calls=%async_computation.9 | async-start | bytes 2654208 | tf_op jit(solution)/shard_map/all_gather | solution.py:152
  305.4 99.2 %reduce-scatter.8.cloned.1.call-start = ((), (), s32[]{:S(2)}) async-start(), calls=%async_computation.10 | async-start | bytes 2654208 | tf_op jit(solution)/shard_map/reduce_scatter | solution.py:158
  351.4 55.8 %copy-start.13 = (s32[3]{0:T(128)S(1)}, s32[3]{0:T(128)}, u32[]{:S(2)}) copy-start(s32[3]{0:T(128)} %param.24) | copy-start | bytes 40
  351.4 133.7 %copy-start.12 = (s32[3]{0:T(128)S(1)}, s32[3]{0:T(128)}, u32[]{:S(2)}) copy-start(s32[3]{0:T(128)} %param.22) | copy-start | bytes 40
  404.7 1.9 copy-start.8
  406.9 1.3 collective-permute-start
Sparse Core Ops, SparseCore 0:
  17.9 33.1 all-gather.5
  68.9 25.8 all-gather.7
  96.6 27.7 all-gather.9
  170.9 29.1 reduce-scatter.3
  203.5 29.1 all-gather.11
  272.9 27.2 reduce-scatter.5
  305.6 30.3 all-gather.13
  351.5 53.1 reduce-scatter.7
where the time goes:
time: 496 us; the launch traced here: 494 us
  waiting for transfers between devices  230 us (46%)
  blocking collectives  103 us (21%)
  local copies, waits for them, and re-layouts  52.3 us (11%)
  matrix products  51.6 us (10%)
  other arithmetic  39.9 us (8%)
  between operations  15.8 us (3%)
    reduce_scatter x2, waiting for transfers between devices, scatter_project(): lax.psum_scatter(jnp.dot(mixed, weight, preferred_element_type=jnp.float3...  56.5 us
    reduce_scatter x1, waiting for transfers between devices, feed_forward(): lax.psum_scatter(jnp.dot(activated, out_weight, preferred_element_type=jn...  53.3 us
    all_gather x2, waiting for transfers between devices, gather_project(): lax.all_gather(row_block, 'tp', axis=0, tiled=True)  40.9 us
    psum x1, blocking collectives, shards(): square_sums = lax.psum(square_sums, ('req', 'tp'))  39.9 us
    pmax x1, blocking collectives, shards(): peak_speed = lax.pmax(peak_speed, ('req', 'tp'))  36.8 us
    all_gather x1, waiting for transfers between devices, feed_forward(): lax.all_gather(ffn_rows, ('cfg', 'tp'), axis=0, tiled=True)  30.2 us
    all_gather x1, waiting for transfers between devices, shards(): lax.all_gather(value_rows, 'req', axis=0, tiled=True)  27.5 us
    all_gather x1, waiting for transfers between devices, shards(): lax.all_gather(key_rows, 'req', axis=0, tiled=True)  20.6 us
  transfers between devices with their start and end apart: 9, of which 9 were waited for; matrix products, arithmetic and copies ran while one was open for 6% of the time, Pallas kernels for 0%

commit v1 on v0

v1 whole, which is shorter than its diff:
```python
import functools

import jax
import jax.numpy as jnp
from jax import lax
from jax.experimental import pallas as pl
from jax.experimental.pallas import tpu as pltpu
from jax.sharding import PartitionSpec as P

HEADS = 12
HD = 128
STEPS = 50

guide_scale = 5.0
rescale_mix = 0.7
flow_shift = 5.0
norm_eps = 1e-06
stat_eps = 1e-05

MESH = pl.DeviceIdType.MESH
BF = jnp.bfloat16
F32 = jnp.float32
VMEM_LIMIT = 48 << 20


def peer_at(axis, offset):
    return lax.rem(lax.axis_index(axis) + offset, lax.axis_size(axis))


def greet(peers):
    barrier = pltpu.get_barrier_semaphore()
    for device in peers:
        pl.semaphore_signal(barrier, inc=1, device_id=device, device_id_type=MESH)
    pl.semaphore_wait(barrier, len(peers))


def others(axis):
    return [{axis: peer_at(axis, offset)} for offset in range(1, lax.axis_size(axis))]


def remote(source, target, send, recv, device):
    return pltpu.make_async_remote_copy(
        src_ref=source,
        dst_ref=target,
        send_sem=send,
        recv_sem=recv,
        device_id=device,
        device_id_type=MESH,
    )


def layer_norm(values):
    average = jnp.mean(values, axis=-1, keepdims=True)
    centered = values - average
    spread = jnp.mean(centered * centered, axis=-1, keepdims=True)
    return centered * lax.rsqrt(spread + norm_eps)


def request_bounds(counts):
    ends = []
    total = jnp.int32(0)
    for r in range(counts.shape[0]):
        total = total + counts[r]
        ends.append(total)
    return ends


def request_column(first, rows, ends):
    position = first + lax.broadcasted_iota(jnp.int32, (rows, 1), 0)
    request = jnp.zeros((rows, 1), jnp.int32)
    for end in ends[:-1]:
        request = request + jnp.where(position >= end, 1, 0)
    return request


def pick(request, choices):
    value = choices[0]
    for r in range(1, len(choices)):
        value = jnp.where(request == r, choices[r], value)
    return value


def mod_rows(mod, request, k):
    return pick(request, [mod[r, k : k + 1, :] for r in range(mod.shape[0])])


def dot(a, b):
    return jnp.dot(a, b, preferred_element_type=F32)


def dot_t(a, b):
    return lax.dot_general(a, b, (((1,), (1,)), ((), ())), preferred_element_type=F32)


def keep_columns(cols):
    if cols * lax.axis_size("tp") <= HEADS * HD:
        return None
    place = lax.axis_index("tp") * cols + lax.broadcasted_iota(jnp.int32, (1, cols), 1)
    return jnp.where(place < HEADS * HD, 1.0, 0.0).astype(F32)


def kept(values, keep):
    return values if keep is None else values * keep


def columns_to_rows(columns):
    rows = columns[0].shape[0]
    lane = lax.broadcasted_iota(jnp.int32, (rows, HD), 1)
    wide = jnp.zeros((rows, HD), F32)
    for i, column in enumerate(columns):
        wide = jnp.where(lane == i, column, wide)
    return jnp.transpose(wide)[:8]


def rows_to_columns(values):
    cols = values.shape[1]
    tall = jnp.concatenate([values, jnp.zeros((HD - 8, cols), F32)], axis=0)
    return jnp.transpose(tall)


def spread_tp(source_of, target_of, send, recv):
    copies = []
    for offset in range(1, lax.axis_size("tp")):
        copy = remote(
            source_of(offset),
            target_of(offset),
            send.at[offset],
            recv.at[offset],
            {"tp": peer_at("tp", offset)},
        )
        copy.start()
        copies.append(copy)
    return copies


def gather_tp(buffer, send, recv):
    me = lax.axis_index("tp")
    return spread_tp(lambda o: buffer.at[me], lambda o: buffer.at[me], send, recv)


def scatter_sum(mix, weight, part, landed, send, recv):
    parts = lax.axis_size("tp")
    copies = []
    for offset in list(range(1, parts)) + [0]:
        target = peer_at("tp", offset)
        part[offset] = dot(mix[target], weight[...]).astype(BF)
        if offset:
            copy = remote(
                part.at[offset],
                landed.at[offset],
                send.at[offset],
                recv.at[offset],
                {"tp": target},
            )
            copy.start()
            copies.append(copy)
    total = part[0].astype(F32)
    for offset, copy in enumerate(copies, 1):
        copy.wait_recv()
        total = total + landed[offset].astype(F32)
    for copy in copies:
        copy.wait_send()
    return total


def add_keys(query, key, value, mask, numer, denom, head):
    cols = slice(head * HD, (head + 1) * HD)
    scores = dot_t(query, key) * HD ** (-0.5)
    weights = jnp.where(mask, jnp.exp(scores), 0.0)
    lanes = denom[head]
    for start in range(0, weights.shape[1], HD):
        lanes = lanes + weights[:, start : start + HD]
    denom[head] = lanes
    numer[:, cols] = numer[:, cols] + dot(weights.astype(BF), value)


def finish(numer, denom, mix, keep):
    parts, rows, width = mix.shape
    for head in range(width // HD):
        cols = slice(head * HD, (head + 1) * HD)
        total = jnp.sum(denom[head], axis=1, keepdims=True)
        mixed = numer[:, cols] / total
        if keep is not None:
            mixed = mixed * keep[:, cols]
        mix[:, :, cols] = mixed.astype(BF).reshape(parts, rows, HD)


def self_kernel(
    counts, mod, states, qkv, gains, out_weight, hidden,
    rows_all, squares, keys, values, query, numer, denom, mix, part, landed,
    ag_send, ag_recv, sq_send, sq_recv, k_send, k_recv, v_send, v_recv, rs_send, rs_recv,
):
    greet(others("tp") + others("req"))
    rows, width = states.shape
    cols = out_weight.shape[0]
    parts, blocks = lax.axis_size("tp"), lax.axis_size("req")
    tp, req = lax.axis_index("tp"), lax.axis_index("req")
    block_rows = rows * parts
    ends = request_bounds(counts)
    request = request_column((req * parts + tp) * rows, rows, ends)
    keep = keep_columns(cols)
    rows_all[tp] = (
        layer_norm(states[...]) * (1.0 + mod_rows(mod, request, 1)) + mod_rows(mod, request, 0)
    ).astype(BF)
    pending = gather_tp(rows_all, ag_send, ag_recv)
    numer[...] = jnp.zeros_like(numer)
    denom[...] = jnp.zeros_like(denom)
    for copy in pending:
        copy.wait_recv()
    full = rows_all[...].reshape(block_rows, width)
    raw_q = kept(dot(full, qkv[:, :cols]), keep)
    raw_k = kept(dot(full, qkv[:, cols : 2 * cols]), keep)
    squares[tp] = columns_to_rows(
        [
            jnp.sum(raw_q * raw_q, axis=1, keepdims=True),
            jnp.sum(raw_k * raw_k, axis=1, keepdims=True),
        ]
    )
    square_copies = gather_tp(squares, sq_send, sq_recv)
    values[req] = dot(full, qkv[:, 2 * cols :]).astype(BF)

    def block_copy(buffer, send, recv, offset):
        return remote(
            buffer.at[req],
            buffer.at[req],
            send.at[offset],
            recv.at[offset],
            {"req": lax.rem(req + offset, blocks)},
        )

    def send_values(offset, carry):
        block_copy(values, v_send, v_recv, offset).start()
        return carry

    def send_keys(offset, carry):
        block_copy(keys, k_send, k_recv, offset).start()
        return carry

    lax.fori_loop(1, blocks, send_values, 0)
    for copy in square_copies:
        copy.wait_recv()
    sums = squares[0]
    for i in range(1, parts):
        sums = sums + squares[i]
    scale = lax.rsqrt(rows_to_columns(sums) / width + norm_eps)
    keys[req] = (raw_k * scale[:, 1:2] * gains[1:2, :]).astype(BF)
    lax.fori_loop(1, blocks, send_keys, 0)
    query[...] = (raw_q * scale[:, 0:1] * gains[0:1, :]).astype(BF)

    query_request = request_column(req * block_rows, block_rows, ends)
    lows = pick(query_request, [jnp.int32(0)] + ends[:-1])
    highs = pick(query_request, ends)

    def attend(slot):
        place = slot * block_rows + lax.broadcasted_iota(jnp.int32, (1, block_rows), 1)
        mask = (place >= lows) & (place < highs)
        for head in range(cols // HD):
            span = slice(head * HD, (head + 1) * HD)
            add_keys(
                query[:, span], keys[slot, :, span], values[slot, :, span], mask, numer, denom, head
            )

    attend(req)

    def visit(offset, carry):
        block_copy(keys, k_send, k_recv, offset).wait_recv()
        block_copy(values, v_send, v_recv, offset).wait_recv()
        attend(lax.rem(req + blocks - offset, blocks))
        return carry

    lax.fori_loop(1, blocks, visit, 0)
    finish(numer, denom, mix, keep)
    delta = scatter_sum(mix, out_weight, part, landed, rs_send, rs_recv)
    hidden[...] = states[...] + mod_rows(mod, request, 2) * delta

    def drain(offset, carry):
        block_copy(keys, k_send, k_recv, offset).wait_send()
        block_copy(values, v_send, v_recv, offset).wait_send()
        return carry

    lax.fori_loop(1, blocks, drain, 0)
    for copy in pending + square_copies:
        copy.wait_send()


def cross_kernel(
    counts, lens, states, gain, query_weight, gains, text, out_weight, hidden,
    rows_all, squares, text_squares, text_keys, numer, denom, mix, part, landed,
    ag_send, ag_recv, sq_send, sq_recv, tx_send, tx_recv, rs_send, rs_recv,
):
    greet(others("tp"))
    rows, width = states.shape
    cols = out_weight.shape[0]
    requests, slots = text.shape[0], text.shape[2]
    parts = lax.axis_size("tp")
    tp, req = lax.axis_index("tp"), lax.axis_index("req")
    block_rows = rows * parts
    ends = request_bounds(counts)
    keep = keep_columns(cols)
    rows_all[tp] = (layer_norm(states[...]) * gain[...]).astype(BF)
    pending = gather_tp(rows_all, ag_send, ag_recv)
    sums = []
    for r in range(requests):
        raw = kept(text[r, 0].astype(F32), keep)
        sums.append(jnp.sum(raw * raw, axis=1, keepdims=True))
    text_squares[tp] = columns_to_rows(sums)
    text_copies = gather_tp(text_squares, tx_send, tx_recv)
    numer[...] = jnp.zeros_like(numer)
    denom[...] = jnp.zeros_like(denom)
    for copy in text_copies:
        copy.wait_recv()
    total = text_squares[0]
    for i in range(1, parts):
        total = total + text_squares[i]
    scale = lax.rsqrt(rows_to_columns(total) / width + norm_eps)
    for r in range(requests):
        raw = kept(text[r, 0].astype(F32), keep)
        text_keys[r] = (raw * scale[:, r : r + 1] * gains[3:4, :]).astype(BF)
    for copy in pending:
        copy.wait_recv()
    raw_q = kept(dot(rows_all[...].reshape(block_rows, width), query_weight[...]), keep)
    squares[tp] = columns_to_rows([jnp.sum(raw_q * raw_q, axis=1, keepdims=True)])
    square_copies = gather_tp(squares, sq_send, sq_recv)
    for copy in square_copies:
        copy.wait_recv()
    total = squares[0]
    for i in range(1, parts):
        total = total + squares[i]
    scale = lax.rsqrt(rows_to_columns(total) / width + norm_eps)
    query = (raw_q * scale[:, 0:1] * gains[2:3, :]).astype(BF)
    query_request = request_column(req * block_rows, block_rows, ends)
    place = lax.broadcasted_iota(jnp.int32, (1, slots), 1)
    for r in range(requests):
        limit = jnp.where(query_request == r, lens[0, r], 0)
        mask = place < limit
        for head in range(cols // HD):
            span = slice(head * HD, (head + 1) * HD)
            add_keys(
                query[:, span], text_keys[r, :, span], text[r, 1, :, span], mask, numer, denom, head
            )
    finish(numer, denom, mix, keep)
    hidden[...] = states[...] + scatter_sum(mix, out_weight, part, landed, rs_send, rs_recv)
    for copy in pending + text_copies + square_copies:
        copy.wait_send()


def noise_level(step_value):
    fraction = 1.0 - step_value / STEPS
    return flow_shift * fraction / (1.0 + (flow_shift - 1.0) * fraction)


def ffn_kernel(
    chunk, counts, steps, mod, states, in_weight, out_weight, head_weight, latent,
    new_latent, velocity_out, peak_out,
    rows_all, acc, half, from_core, part, landed, speed, stats_tp, stats_req,
    ag_send, ag_recv, fw_send, fw_recv, core_send, core_recv, swap_send, swap_recv,
    rs_send, rs_recv, st_send, st_recv, sr_send, sr_recv,
):
    core, tp, req = lax.axis_index("cfg"), lax.axis_index("tp"), lax.axis_index("req")
    mate = {"cfg": 1 - core}
    greet(others("tp") + others("req") + [mate])
    rows, width = states.shape
    parts, blocks = lax.axis_size("tp"), lax.axis_size("req")
    block_rows = rows * parts
    units = in_weight.shape[0]
    requests = counts.shape[0]
    ends = request_bounds(counts)
    request = request_column((req * parts + tp) * rows, rows, ends)
    mine = rows_all.at[core]
    mine[tp] = (
        layer_norm(states[...]) * (1.0 + mod_rows(mod, request, 4)) + mod_rows(mod, request, 3)
    ).astype(BF)
    pending = gather_tp(mine, ag_send, ag_recv)
    forwards = []

    def forward(offset):
        source = lax.rem(tp + parts - offset, parts)
        copy = remote(
            rows_all.at[core, source],
            rows_all.at[core, source],
            fw_send.at[offset],
            fw_recv.at[offset],
            mate,
        )
        copy.start()
        forwards.append(copy)

    forward(0)
    for offset, copy in enumerate(pending, 1):
        copy.wait_recv()
        forward(offset)

    def work(which):
        full = rows_all[which].reshape(block_rows, width)
        acc[...] = jnp.zeros_like(acc)

        def step(i, carry):
            span = pl.ds(pl.multiple_of(i * chunk, 16), chunk)
            up = dot_t(full, in_weight[span, :])
            act = jax.nn.gelu(up, approximate=True).astype(BF)
            acc[...] = acc[...] + dot(act, out_weight[span, :])
            return carry

        lax.fori_loop(0, units // chunk, step, 0)

    for copy in forwards:
        copy.wait_recv()
    work(1 - core)
    half[...] = acc[...].astype(BF)
    across = remote(half, from_core, core_send, core_recv, mate)
    across.start()
    work(core)
    across.wait_recv()
    copies = []
    for offset in list(range(1, parts)) + [0]:
        target = peer_at("tp", offset)
        span = pl.ds(pl.multiple_of(target * rows, 16), rows)
        total = acc[span, :] + from_core[span, :].astype(F32)
        if offset:
            part[offset] = total.astype(BF)
            copy = remote(
                part.at[offset],
                landed.at[offset],
                rs_send.at[offset],
                rs_recv.at[offset],
                {"tp": target},
            )
            copy.start()
            copies.append(copy)
    for offset, copy in enumerate(copies, 1):
        copy.wait_recv()
        total = total + landed[offset].astype(F32)
    last = states[...] + mod_rows(mod, request, 5) * total
    own = dot(layer_norm(last).astype(BF), head_weight[...])
    speed[0] = own
    swap = remote(speed.at[0], speed.at[1], swap_send, swap_recv, mate)
    swap.start()
    swap.wait()
    other = speed[1]
    cond = jnp.where(core == 0, own, other)
    plain = jnp.where(core == 0, other, own)
    guided = plain + guide_scale * (cond - plain)
    lane = lax.broadcasted_iota(jnp.int32, (8, HD), 1)
    line = lax.broadcasted_iota(jnp.int32, (8, HD), 0)
    pack = jnp.zeros((8, HD), F32)
    per_row = [
        jnp.sum(cond * cond, axis=1, keepdims=True),
        jnp.sum(guided * guided, axis=1, keepdims=True),
        jnp.max(jnp.abs(guided), axis=1, keepdims=True),
    ]
    for r in range(requests):
        for i, column in enumerate(per_row):
            chosen = jnp.where(request == r, column, 0.0)
            if i < 2:
                value = jnp.sum(chosen, axis=0, keepdims=True)
            else:
                value = jnp.max(chosen, axis=0, keepdims=True)
            pack = jnp.where((lane == r) & (line == i), value, pack)

    def combine(buffer):
        total, top = buffer[0], buffer[0]
        for i in range(1, buffer.shape[0]):
            total = total + buffer[i]
            top = jnp.maximum(top, buffer[i])
        return jnp.where(line == 2, top, total)

    stats_tp[tp] = pack
    stat_copies = gather_tp(stats_tp, st_send, st_recv)
    for copy in stat_copies:
        copy.wait_recv()
    stats_req[req] = combine(stats_tp)
    for offset in range(1, blocks):
        copy = remote(
            stats_req.at[req],
            stats_req.at[req],
            sr_send.at[offset],
            sr_recv.at[offset],
            {"req": peer_at("req", offset)},
        )
        copy.start()
        stat_copies.append(copy)
    for copy in stat_copies[parts - 1 :]:
        copy.wait_recv()
    stats = combine(stats_req)
    lanes = lane[:1]
    count = jnp.ones((1, HD), F32)
    step_value = jnp.zeros((1, HD), F32)
    for r in range(requests):
        count = jnp.where(lanes == r, (counts[r] * guided.shape[1]).astype(F32), count)
        step_value = jnp.where(lanes == r, steps[r].astype(F32), step_value)
    cond_rms = jnp.sqrt(stats[0:1] / count + stat_eps)
    guided_rms = jnp.sqrt(stats[1:2] / count + stat_eps)
    factor = rescale_mix * cond_rms / guided_rms + (1.0 - rescale_mix)
    delta_t = noise_level(step_value + 1.0) - noise_level(step_value)
    peak_out[...] = factor * stats[2:3]
    row_factor = pick(request, [factor[:, r : r + 1] for r in range(requests)])
    row_step = pick(request, [delta_t[:, r : r + 1] for r in range(requests)])
    velocity = row_factor * guided
    moved = latent[...] + row_step * velocity
    own_cols = velocity_out.shape[1]
    velocity_out[...] = jnp.where(core == 0, velocity[:, :own_cols], velocity[:, own_cols:])
    new_latent[...] = jnp.where(core == 0, moved[:, :own_cols], moved[:, own_cols:])
    for copy in pending + forwards + copies + stat_copies + [across]:
        copy.wait_send()


def call(body, outs, spaces, scratch, collective, flops):
    return pl.pallas_call(
        body,
        out_shape=outs,
        in_specs=[pl.BlockSpec(memory_space=space) for space in spaces],
        out_specs=jax.tree.map(lambda _: pl.BlockSpec(memory_space=pltpu.VMEM), outs),
        scratch_shapes=scratch,
        compiler_params=pltpu.CompilerParams(
            collective_id=collective, has_side_effects=True, vmem_limit_bytes=VMEM_LIMIT
        ),
        cost_estimate=pl.CostEstimate(flops=flops, bytes_accessed=8 << 20, transcendentals=0),
    )


def shards(
    latent,
    states,
    token_counts,
    text_lens,
    steps_index,
    modulation,
    self_qkv,
    self_out,
    qk_gains,
    cross_query,
    cross_out,
    cross_gain,
    text_kv,
    ffn_in_weight,
    ffn_out_weight,
    head_weight,
):
    rows = latent.shape[0]
    width = head_weight.shape[0]
    cols = self_out.shape[0]
    heads = cols // HD
    parts, blocks = lax.axis_size("tp"), lax.axis_size("req")
    block_rows = rows * parts
    requests, slots = text_kv.shape[1], text_kv.shape[3]
    V, S = pltpu.VMEM, pltpu.SMEM

    def sems(*sizes):
        return [pltpu.SemaphoreType.DMA((size,)) for size in sizes for _ in range(2)]

    wide = pltpu.VMEM((parts, rows, width), BF)
    attention = [
        pltpu.VMEM((block_rows, cols), F32),
        pltpu.VMEM((heads, block_rows, HD), F32),
        pltpu.VMEM((parts, rows, cols), BF),
        wide,
        wide,
    ]
    hidden_shape = jax.ShapeDtypeStruct((rows, width), F32)
    hidden = call(
        self_kernel,
        hidden_shape,
        [S, V, V, V, V, V],
        [
            wide,
            pltpu.VMEM((parts, 8, block_rows), F32),
            pltpu.VMEM((blocks, block_rows, cols), BF),
            pltpu.VMEM((blocks, block_rows, cols), BF),
            pltpu.VMEM((block_rows, cols), BF),
        ]
        + attention
        + sems(parts, parts, blocks, blocks, parts),
        1,
        2 * block_rows * width * cols * 4,
    )(token_counts, modulation, states[0], self_qkv.reshape(width, 3 * cols), qk_gains, self_out)
    hidden = call(
        cross_kernel,
        hidden_shape,
        [S, S, V, V, V, V, V, V],
        [
            wide,
            pltpu.VMEM((parts, 8, block_rows), F32),
            pltpu.VMEM((parts, 8, slots), F32),
            pltpu.VMEM((requests, slots, cols), BF),
        ]
        + attention
        + sems(parts, parts, parts, parts),
        2,
        2 * block_rows * width * cols * 2,
    )(
        token_counts,
        text_lens,
        hidden,
        cross_gain.reshape(1, width),
        cross_query,
        qk_gains,
        text_kv[0],
        cross_out,
    )
    units = ffn_in_weight.shape[0]
    chunk = units // 5 if units % 80 == 0 else units
    out_cols = latent.shape[1] // lax.axis_size("cfg")
    small = jax.ShapeDtypeStruct((rows, out_cols), F32)
    new_latent, velocity, peak = call(
        functools.partial(ffn_kernel, chunk),
        (small, small, jax.ShapeDtypeStruct((1, HD), F32)),
        [S, S, V, V, V, V, V, V],
        [
            pltpu.VMEM((2, parts, rows, width), BF),
            pltpu.VMEM((block_rows, width), F32),
            pltpu.VMEM((block_rows, width), BF),
            pltpu.VMEM((block_rows, width), BF),
            wide,
            wide,
            pltpu.VMEM((2, rows, latent.shape[1]), F32),
            pltpu.VMEM((parts, 8, HD), F32),
            pltpu.VMEM((blocks, 8, HD), F32),
        ]
        + sems(parts, parts)
        + [pltpu.SemaphoreType.DMA] * 4
        + sems(parts, parts, blocks),
        3,
        4 * 2 * block_rows * width * units,
    )(
        token_counts,
        steps_index,
        modulation,
        hidden,
        ffn_in_weight,
        ffn_out_weight,
        head_weight,
        latent,
    )
    return new_latent, velocity, peak[0, :requests]


def solution(mesh):
    in_specs = (
        P(("req", "tp"), None),
        P("cfg", ("req", "tp"), None),
        P(),
        P("cfg", None),
        P(),
        P(),
        P(None, None, "tp"),
        P("tp", None),
        P(None, "tp"),
        P(None, "tp"),
        P("tp", None),
        P(),
        P("cfg", None, None, None, "tp"),
        P(("cfg", "tp"), None),
        P(("cfg", "tp"), None),
        P(),
    )
    out_specs = (P(("req", "tp"), "cfg"), P(("req", "tp"), "cfg"), P())
    return jax.shard_map(shards, mesh=mesh, in_specs=in_specs, out_specs=out_specs, check_vma=False)
```

time: 496 us -> 258 us (0.52)
  Pallas kernels: 0 us -> 238 us
  waiting for transfers between devices: 230 us -> 0 us
  blocking collectives: 103 us -> 0 us
  matrix products: 51.6 us -> 0 us
  other arithmetic: 39.9 us -> 0 us
  local copies, waits for them, and re-layouts: 52.3 us -> 18.4 us
  between operations: 15.8 us -> 0.85 us
    pallas_call x0 -> x3, Pallas kernels: none -> 238 us  [the longest x1 90.4 us: shards(): call(functools.partial(ffn_kernel, chunk), (small, small, jax.ShapeDtypeS...]
    all_gather x5 -> x0, waiting for transfers between devices: 119 us -> none  [the longest x2 40.9 us: gather_project(): lax.all_gather(row_block, 'tp', axis=0, tiled=True)]
    reduce_scatter x3 -> x0, waiting for transfers between devices: 110 us -> none  [the longest x2 56.5 us: scatter_project(): lax.psum_scatter(jnp.dot(mixed, weight, preferred_element_type=jnp.float3...]
    psum x3 -> x0, blocking collectives: 66.7 us -> none  [the longest x1 39.9 us: shards(): square_sums = lax.psum(square_sums, ('req', 'tp'))]
    dot_general x15 -> x0, matrix products: 51.6 us -> none  [the longest x1 15.4 us: feed_forward(): jnp.dot(activated, out_weight, preferred_element_type=jnp.float32)]
    pmax x1 -> x0, blocking collectives: 36.8 us -> none  [shards(): peak_speed = lax.pmax(peak_speed, ('req', 'tp'))]
    convert_element_type x8 -> x0, other arithmetic: 17.8 us -> none  [the longest x3 9.85 us: rms_scale(): (values * lax.rsqrt(square_sum / width + norm_eps)[:, None] * gains).asty...]
    another operation x9 -> x0, local copies, waits for them, and re-layouts: 17.3 us -> none
  transfers between devices with their start and end apart: 9 -> 0, of which waited for: 9 -> 0; matrix products, arithmetic and copies ran while one was open for 6% -> 0% of each run, Pallas kernels for 0% -> 0%
where the time goes in v1:
time: 258 us
  Pallas kernels  238 us (92%)
  local copies, waits for them, and re-layouts  18.4 us (7%)
    pallas_call x1, Pallas kernels, shards(): call(functools.partial(ffn_kernel, chunk), (small, small, jax.ShapeDtypeS...  90.4 us
    pallas_call x1, Pallas kernels, shards(): call(self_kernel, hidden_shape, [S, V, V, V, V, V], [wide, pltpu.VMEM((pa...  79.8 us
    pallas_call x1, Pallas kernels, shards(): call(cross_kernel, hidden_shape, [S, S, V, V, V, V, V, V], [wide, pltpu.V...  68.3 us
    unnamed x35, local copies, waits for them, and re-layouts  13.4 us

profile of v1, /device:TPU:0, one launch (start us, length us, event | category | flops | bytes accessed | tf_op | source)
XLA Modules:
  0.0 257.7 jit_solution(17443740986305314802)
XLA Ops:
  0.6 6.1 %copy.24 = bf16[1536,3,384]{0,2,1:T(8,128)(2,1)} copy(bf16[1536,3,384]{2,0,1:T(8,128)(2,1)} %param.22) | data formatting | bytes 7077888 | tf_op args[6]
  6.7 0.0 copy-start.3
  6.7 0.0 copy-start.5
  6.7 4.4 %copy.25.qkv = bf16[1536,1152]{1,0:T(8,128)(2,1)S(1)} copy(bf16[1536,1152]{0,1:T(8,128)(2,1)} %bitcast.7) | data formatting | bytes 7077888 | tf_op jit(solution)/shard_map/reshape | solution.py:575
  11.1 0.0 copy-start
  11.1 0.0 copy-start.1
  11.1 0.0 copy-start.2
  11.1 0.0 copy-start.4
  11.1 0.0 copy-done.3
  11.2 0.0 copy-done.5
  11.2 0.0 copy-start.7
  11.2 1.4 copy-done.7
  12.6 0.0 copy-start.8
  12.6 1.4 copy-done.8
  14.0 0.0 copy-start.9
  14.0 0.9 copy-done.9
  14.9 0.0 copy-start.14
  14.9 79.8 %shard_map.175.states = f32[96,1536]{1,0:T(8,128)S(1)} custom-call(s32[3]{0:T(128)S(1)} %copy-done.5, f32[3,6,1536]{2,1,0:T(8,128)S(1)} %copy-done.9, f32[96,1536]{1,0:T(8,128)S(1)} %bitcast.6, bf16[1536,1152]{1,0:T(8,128)(2,1)S(1)} %copy.25.qkv, f32[4,384]{1,0:T(4,128)S(1)} %copy-done.3, bf16[384,1536]{1,0:T(8,128)(2,1)S(1)} %copy-done.7), custom_call_target="tpu_custom_call" | custom-call | flops 1811939328 | bytes 8388608 | tf_op jit(solution)/shard_map/pallas_call | solution.py:560
  94.7 0.0 copy-done.14
  94.7 0.0 copy-start.12
  94.7 0.0 copy-start.13
  94.7 0.0 copy-start.10
  94.7 0.0 copy-start.11
  94.7 0.0 copy-done
  94.8 0.0 copy-done.1
  94.8 0.0 copy-done.2
  94.8 0.0 copy-done.4
  94.8 68.3 %shard_map.176.states = f32[96,1536]{1,0:T(8,128)S(1)} custom-call(s32[3]{0:T(128)S(1)} %copy-done.5, s32[1,3]{1,0:T(1,128)S(1)} %copy-done.4, f32[96,1536]{1,0:T(8,128)S(1)} %shard_map.175.states, f32[1,1536]{1,0:T(1,128)S(1)} %reshape.13.gain, bf16[1536,384]{1,0:T(8,128)(2,1)S(1)} %copy-done.1, f32[4,384]{1,0:T(4,128)S(1)} %copy-done.3, ...), custom_call_target="tpu_custom_call" | custom-call | flops 905969664 | bytes 8388608 | tf_op jit(solution)/shard_map/pallas_call | solution.py:576
  163.1 0.0 copy-done.12
  163.1 0.2 copy.26.head_weight
  163.3 0.0 copy-done.13
  163.3 0.1 copy.27.latent
  163.4 0.0 copy-done.10
  163.4 0.0 copy-done.11
  163.4 0.0 copy-start.6
  163.4 2.0 copy-done.6
  165.4 90.4 %shard_map.177 = (f32[96,32]{1,0:T(8,128)S(1)}, f32[96,32]{1,0:T(8,128)S(1)}, f32[1,128]{1,0:T(1,128)S(1)}) custom-call(s32[3]{0:T(128)S(1)} %copy-done.5, s32[3]{0:T(128)S(1)} %copy-done.11, f32[3,6,1536]{2,1,0:T(8,128)S(1)} %copy-done.10, f32[96,1536]{1,0:T(8,128)S(1)} %shard_map.176.states, bf16[1120,1536]{1,0:T(8,128)(2,1)S(1)} %copy-done.6, ...), custom_call_target="tpu_custom_call" | custom-call | flops 5284823040 | bytes 8388608 | tf_op jit(solution)/shard_map/pallas_call | solution.py:604
  255.8 0.7 copy.28
  256.5 0.7 copy.29
  257.2 0.5 slice_bitcast_fusion
  (1 shorter events, 0.0 us)
Async XLA Ops:
  6.7 4.5 %copy-start.3 = (f32[4,384]{1,0:T(4,128)S(1)}, f32[4,384]{1,0:T(4,128)}, u32[]{:S(2)}) copy-start(f32[4,384]{1,0:T(4,128)} %gains.3) | copy-start | bytes 18436
  6.7 4.5 %copy-start.5 = (s32[3]{0:T(128)S(1)}, s32[3]{0:T(128)}, u32[]{:S(2)}) copy-start(s32[3]{0:T(128)} %counts.5) | copy-start | bytes 40
  11.1 83.7 %copy-start = (bf16[1,3,2,512,384]{4,3,2,1,0:T(8,128)(2,1)S(1)}, bf16[1,3,2,512,384]{4,3,2,1,0:T(8,128)(2,1)}, u32[]{:S(2)}) copy-start(bf16[1,3,2,512,384]{4,3,2,1,0:T(8,128)(2,1)} %param.28) | copy-start | bytes 7077892
  11.1 83.6 %copy-start.1 = (bf16[1536,384]{1,0:T(8,128)(2,1)S(1)}, bf16[1536,384]{1,0:T(8,128)(2,1)}, u32[]{:S(2)}) copy-start(bf16[1536,384]{1,0:T(8,128)(2,1)} %query_weight.1) | copy-start | bytes 3538948
  11.1 83.6 %copy-start.2 = (bf16[384,1536]{1,0:T(8,128)(2,1)S(1)}, bf16[384,1536]{1,0:T(8,128)(2,1)}, u32[]{:S(2)}) copy-start(bf16[384,1536]{1,0:T(8,128)(2,1)} %out_weight.4) | copy-start | bytes 3538948
  11.1 83.6 %copy-start.4 = (s32[1,3]{1,0:T(1,128)S(1)}, s32[1,3]{1,0:T(1,128)}, u32[]{:S(2)}) copy-start(s32[1,3]{1,0:T(1,128)} %lens.1) | copy-start | bytes 40
  11.2 1.4 copy-start.7
  12.6 1.4 copy-start.8
  14.0 0.9 copy-start.9
  14.9 79.8 %copy-start.14 = (f32[1536]{0:T(1024)S(1)}, f32[1536]{0:T(1024)}, u32[]{:S(2)}) copy-start(f32[1536]{0:T(1024)} %param.27) | copy-start | bytes 18436
  94.7 68.4 %copy-start.12 = (bf16[1536,64]{0,1:T(8,128)(2,1)S(1)}, bf16[1536,64]{0,1:T(8,128)(2,1)}, u32[]{:S(2)}) copy-start(bf16[1536,64]{0,1:T(8,128)(2,1)} %param.31) | copy-start | bytes 589828
  94.7 68.6 %copy-start.13 = (f32[96,64]{0,1:T(8,128)S(1)}, f32[96,64]{0,1:T(8,128)}, u32[]{:S(2)}) copy-start(f32[96,64]{0,1:T(8,128)} %param.16) | copy-start | bytes 73732
  94.7 68.7 %copy-start.10 = (f32[3,6,1536]{2,1,0:T(8,128)S(1)}, f32[3,6,1536]{2,1,0:T(8,128)}, u32[]{:S(2)}) copy-start(f32[3,6,1536]{2,1,0:T(8,128)} %mod.3) | copy-start | bytes 331780
  94.7 68.7 %copy-start.11 = (s32[3]{0:T(128)S(1)}, s32[3]{0:T(128)}, u32[]{:S(2)}) copy-start(s32[3]{0:T(128)} %steps.1) | copy-start | bytes 40
  163.4 2.0 copy-start.6

commit v2 on v1

v2 whole, which is shorter than its diff:
```python
import functools
import types

import jax
import jax.numpy as jnp
from jax import lax
from jax.experimental import pallas as pl
from jax.experimental.pallas import tpu as pltpu
from jax.sharding import PartitionSpec as P

HEADS = 12
HD = 128
STEPS = 50

guide_scale = 5.0
rescale_mix = 0.7
flow_shift = 5.0
norm_eps = 1e-06
stat_eps = 1e-05

MESH = pl.DeviceIdType.MESH
BF = jnp.bfloat16
F32 = jnp.float32
VMEM_LIMIT = 60 << 20


def peer_at(axis, offset):
    return lax.rem(lax.axis_index(axis) + offset, lax.axis_size(axis))


def greet(peers):
    barrier = pltpu.get_barrier_semaphore()
    for device in peers:
        pl.semaphore_signal(barrier, inc=1, device_id=device, device_id_type=MESH)
    pl.semaphore_wait(barrier, len(peers))


def others(axis):
    return [{axis: peer_at(axis, offset)} for offset in range(1, lax.axis_size(axis))]


def remote(source, target, send, recv, device):
    return pltpu.make_async_remote_copy(
        src_ref=source,
        dst_ref=target,
        send_sem=send,
        recv_sem=recv,
        device_id=device,
        device_id_type=MESH,
    )


def layer_norm(values):
    average = jnp.mean(values, axis=-1, keepdims=True)
    centered = values - average
    spread = jnp.mean(centered * centered, axis=-1, keepdims=True)
    return centered * lax.rsqrt(spread + norm_eps)


def request_bounds(counts):
    ends = []
    total = jnp.int32(0)
    for r in range(counts.shape[0]):
        total = total + counts[r]
        ends.append(total)
    return ends


def pick(request, choices):
    value = choices[0]
    for r in range(1, len(choices)):
        value = jnp.where(request == r, choices[r], value)
    return value


def mod_rows(mod, request, k):
    return pick(request, [mod[r, k : k + 1, :] for r in range(mod.shape[0])])


def dot(a, b):
    return jnp.dot(a, b, preferred_element_type=F32)


def dot_t(a, b):
    return lax.dot_general(a, b, (((1,), (1,)), ((), ())), preferred_element_type=F32)


def keep_columns(cols):
    if cols * lax.axis_size("tp") <= HEADS * HD:
        return None
    place = lax.axis_index("tp") * cols + lax.broadcasted_iota(jnp.int32, (1, cols), 1)
    return jnp.where(place < HEADS * HD, 1.0, 0.0).astype(F32)


def kept(values, keep):
    return values if keep is None else values * keep


def columns_to_rows(columns):
    rows = columns[0].shape[0]
    lane = lax.broadcasted_iota(jnp.int32, (rows, HD), 1)
    wide = jnp.zeros((rows, HD), F32)
    for i, column in enumerate(columns):
        wide = jnp.where(lane == i, column, wide)
    return jnp.transpose(wide)[:8]


def rows_to_columns(values):
    cols = values.shape[1]
    tall = jnp.concatenate([values, jnp.zeros((HD - 8, cols), F32)], axis=0)
    return jnp.transpose(tall)


class Gather:
    def __init__(self, buffer, send, recv, chunk, relayed=False):
        self.tp, self.parts = lax.axis_index("tp"), lax.axis_size("tp")
        self.line = relayed and self.parts == 4
        self.inner = (self.tp == 1) | (self.tp == 2)
        self.buffer, self.send, self.recv, self.chunk = buffer, send, recv, chunk
        self.copies = {o: self.copy(self.tp, o) for o in range(1, self.parts)}
        self.onward = None
        for offset in sorted(self.copies, key=lambda o: (o != 2, o)):
            self.unless(self.line and self.skips_send(offset), self.copies[offset].start)

    def copy(self, source, offset):
        return remote(
            self.buffer.at[source],
            self.buffer.at[source],
            self.send.at[self.chunk, offset],
            self.recv.at[self.chunk, offset],
            {"tp": lax.rem(self.tp + offset, self.parts)},
        )

    def skips_send(self, offset):
        return {1: self.tp == 3, 3: self.tp == 0}.get(offset, False)

    def unless(self, condition, action):
        if condition is False:
            action()
        else:
            pl.when(jnp.logical_not(condition))(action)

    def relay(self):
        if not self.line or self.onward is not None:
            return
        source = 3 * (2 - self.tp)
        self.onward = remote(
            self.buffer.at[source],
            self.buffer.at[source],
            self.send.at[self.chunk, 0],
            self.recv.at[self.chunk, 2 * self.tp - 1],
            {"tp": 3 * (self.tp - 1)},
        )

        @pl.when(self.inner)
        def _():
            self.copies[2].wait_recv()
            self.onward.start()

    def wait_one(self, offset):
        self.relay()
        skip = self.inner if self.line and offset == 2 else False
        self.unless(skip, self.copies[offset].wait_recv)

    def wait_recv(self):
        for offset in self.copies:
            self.wait_one(offset)

    def wait_send(self):
        for offset, copy in self.copies.items():
            self.unless(self.line and self.skips_send(offset), copy.wait_send)
        if self.line:
            pl.when(self.inner)(self.onward.wait_send)


class Scatter:
    def __init__(self, part, landed, send, recv, chunk):
        self.tp, self.parts = lax.axis_index("tp"), lax.axis_size("tp")
        self.line = self.parts == 4
        self.inner = (self.tp == 1) | (self.tp == 2)
        self.part, self.landed = part, landed
        self.copies, self.vias, self.relayed = {}, {}, False
        self.first = None
        for offset in sorted(range(1, self.parts), key=lambda o: (o == 2, -o)):
            target = lax.rem(self.tp + offset, self.parts)
            copy = remote(
                part.at[target],
                landed.at[offset],
                send.at[chunk, offset],
                recv.at[chunk, offset],
                {"tp": target},
            )
            self.copies[offset] = copy
            if not self.line:
                copy.start()
            elif offset == 2:
                pl.when(jnp.logical_not(self.inner))(copy.start)
            else:
                far = self.far(offset)
                via = remote(
                    part.at[target],
                    landed.at[0],
                    send.at[chunk, offset],
                    recv.at[chunk, 0],
                    {"tp": 1 if offset == 3 else 2},
                )
                self.vias[offset] = via
                pl.when(far)(via.start)
                pl.when(jnp.logical_not(far))(copy.start)

    def far(self, offset):
        return self.tp == (0 if offset == 3 else 3)

    def relay(self):
        if not self.line or self.relayed:
            return
        self.relayed = True
        target = lax.rem(self.tp + 2, self.parts)

        @pl.when(self.inner)
        def _():
            self.vias[3].wait_recv()
            joined = self.part[target].astype(F32) + self.landed[0].astype(F32)
            self.part[target] = joined.astype(BF)
            self.copies[2].start()

        for offset in (1, 3):

            @pl.when(self.tp == (0 if offset == 1 else 3))
            def _(offset=offset):
                self.landed[offset] = jnp.zeros(self.landed.shape[1:], BF)

    def total(self):
        self.relay()
        total = self.part[self.tp].astype(F32)
        for offset in sorted(self.copies):
            wait = self.copies[offset].wait_recv
            if self.line and offset != 2:
                pl.when(self.tp != (0 if offset == 1 else 3))(wait)
            else:
                wait()
            total = total + self.landed[offset].astype(F32)
        return total

    def wait_send(self):
        for copy in self.copies.values():
            copy.wait_send()


def placed(index, segments):
    place = index
    for start, first in segments:
        place = jnp.where(index >= start, index - start + first, place)
    return place


def request_at(position, ends):
    request = jnp.zeros(position.shape, jnp.int32)
    for end in ends[:-1]:
        request = request + jnp.where(position >= end, 1, 0)
    return request


def add_all(buffer):
    total = buffer[0]
    for i in range(1, buffer.shape[0]):
        total = total + buffer[i]
    return total


def row_scale(squares, width):
    return lax.rsqrt(rows_to_columns(add_all(squares)) / width + norm_eps)


def square_sums(values):
    return jnp.sum(values * values, axis=1, keepdims=True)


def add_keys(query, key, value, mask, numer, denom, head, first=0):
    rows = slice(first, first + query.shape[0])
    cols = slice(head * HD, (head + 1) * HD)
    scores = dot_t(query, key) * HD ** (-0.5)
    weights = jnp.where(mask, jnp.exp(scores), 0.0)
    lanes = denom[head, rows, :]
    for start in range(0, weights.shape[1], HD):
        lanes = lanes + weights[:, start : start + HD]
    denom[head, rows, :] = lanes
    numer[rows, cols] = numer[rows, cols] + dot(weights.astype(BF), value)


def finish(numer, denom, mix, keep, first):
    parts, size, width = mix.shape
    rows = slice(first, first + parts * size)
    for head in range(width // HD):
        cols = slice(head * HD, (head + 1) * HD)
        total = jnp.sum(denom[head, rows, :], axis=1, keepdims=True)
        mixed = numer[rows, cols] / total
        if keep is not None:
            mixed = mixed * keep[:, cols]
        mix[:, :, cols] = mixed.astype(BF).reshape(parts, size, HD)


def noise_level(step_value):
    fraction = 1.0 - step_value / STEPS
    return flow_shift * fraction / (1.0 + (flow_shift - 1.0) * fraction)


def block_kernel(
    sizes, chunk_units, names, chunk_names, *refs,
):
    ref = types.SimpleNamespace(**dict(zip(names, refs)))
    rest = refs[len(names) :]
    per = []
    for c in range(len(sizes)):
        mine = rest[c * len(chunk_names) : (c + 1) * len(chunk_names)]
        per.append(types.SimpleNamespace(**dict(zip(chunk_names, mine, strict=True))))
    counts, lens, steps, mod, states = ref.counts, ref.lens, ref.steps, ref.mod, ref.states
    gains = ref.gains
    rows, width = states.shape
    cols = ref.self_out.shape[0]
    core, tp, req = lax.axis_index("cfg"), lax.axis_index("tp"), lax.axis_index("req")
    parts, blocks = lax.axis_size("tp"), lax.axis_size("req")
    block_rows = rows * parts
    heads = cols // HD
    requests = counts.shape[0]
    mate = {"cfg": 1 - core}

    def fetch(i, source, target):
        copy = pltpu.make_async_copy(source, target, ref.fetch_sem.at[i])
        copy.start()
        return copy

    fetches = types.SimpleNamespace(
        qkv=fetch(0, ref.qkv, ref.v_qkv),
        text=fetch(1, ref.text, ref.v_text),
        self_out=fetch(2, ref.self_out, ref.v_self_out),
        cross_query=fetch(3, ref.cross_query, ref.v_cross_query),
        cross_out=fetch(4, ref.cross_out, ref.v_cross_out),
        ffn_in=fetch(5, ref.ffn_in, ref.v_ffn_in),
        ffn_out=fetch(6, ref.ffn_out, ref.v_ffn_out),
    )
    greet(others("tp") + others("req") + [mate])

    starts = [sum(sizes[:c]) for c in range(len(sizes))]
    chunks = range(len(sizes))
    spans = [slice(starts[c], starts[c] + sizes[c]) for c in chunks]
    key_starts = [parts * start for start in starts]
    segments = [
        [(t * sizes[c], t * rows + starts[c]) for t in range(parts)] for c in chunks
    ]
    all_segments = [
        (key_starts[c] + start, first) for c in chunks for start, first in segments[c]
    ]
    ends = request_bounds(counts)
    row_first = (req * parts + tp) * rows
    request = [
        request_at(
            row_first + starts[c] + lax.broadcasted_iota(jnp.int32, (sizes[c], 1), 0), ends
        )
        for c in chunks
    ]
    keep = keep_columns(cols)
    done = []

    rows_self = [per[c].rows_self for c in chunks]
    gathers = []
    for c in chunks:
        rows_self[c][tp] = (
            layer_norm(states[spans[c], :]) * (1.0 + mod_rows(mod, request[c], 1))
            + mod_rows(mod, request[c], 0)
        ).astype(BF)
        gathers.append(Gather(rows_self[c], ref.ag_send, ref.ag_recv, c, True))
    numer, denom = ref.numer, ref.denom
    numer[...] = jnp.zeros_like(numer)
    denom[...] = jnp.zeros_like(denom)

    fetches.text.wait()
    text, text_squares, text_keys = ref.v_text, ref.text_squares, ref.text_keys
    text_squares[tp] = columns_to_rows(
        [square_sums(kept(text[r, 0].astype(F32), keep)) for r in range(requests)]
    )
    text_copies = Gather(text_squares, ref.tx_send, ref.tx_recv, 0)

    fetches.qkv.wait()
    qkv, keys, values, query = ref.v_qkv, ref.keys, ref.values, ref.query

    def block_copy(buffer, send, recv, c, offset):
        span = pl.ds(key_starts[c], parts * sizes[c])
        return remote(
            buffer.at[req, span],
            buffer.at[req, span],
            send.at[c, offset],
            recv.at[c, offset],
            {"req": lax.rem(req + offset, blocks)},
        )

    def key_copy(c, offset):
        return block_copy(keys, ref.k_send, ref.k_recv, c, offset)

    def value_copy(c, offset):
        return block_copy(values, ref.v_send, ref.v_recv, c, offset)

    def start_all(make, c):
        def body(offset, carry):
            make(c, offset).start()
            return carry

        lax.fori_loop(1, blocks, body, 0)

    raws, square_copies = [], []
    for c in chunks:
        gathers[c].wait_recv()
        full = rows_self[c][...].reshape(parts * sizes[c], width)
        key_span = slice(key_starts[c], key_starts[c] + parts * sizes[c])
        values[req, key_span, :] = dot(full, qkv[2]).astype(BF)
        start_all(value_copy, c)
        for later in gathers[c + 1 :]:
            later.relay()
        raw_k = kept(dot(full, qkv[1]), keep)
        raw_q = kept(dot(full, qkv[0]), keep)
        ref.raw_k[key_span, :] = raw_k
        ref.raw_q[key_span, :] = raw_q
        squares = per[c].squares_self
        squares[tp] = columns_to_rows([square_sums(raw_q), square_sums(raw_k)])
        square_copies.append(Gather(squares, ref.sq_send, ref.sq_recv, c))
    for c in chunks:
        square_copies[c].wait_recv()
        key_span = slice(key_starts[c], key_starts[c] + parts * sizes[c])
        scale = row_scale(per[c].squares_self, width)
        keys[req, key_span, :] = (ref.raw_k[key_span, :] * scale[:, 1:2] * gains[1:2, :]).astype(BF)
        start_all(key_copy, c)
        query[key_span, :] = (ref.raw_q[key_span, :] * scale[:, 0:1] * gains[0:1, :]).astype(BF)
    done += gathers + square_copies

    key_place = placed(lax.broadcasted_iota(jnp.int32, (1, block_rows), 1), all_segments)
    query_request = request_at(
        req * block_rows
        + placed(lax.broadcasted_iota(jnp.int32, (block_rows, 1), 0), all_segments),
        ends,
    )
    lows = pick(query_request, [jnp.int32(0)] + ends[:-1])
    highs = pick(query_request, ends)

    def attend(slot):
        place = slot * block_rows + key_place
        mask = (place >= lows) & (place < highs)
        for head in range(heads):
            span = slice(head * HD, (head + 1) * HD)
            add_keys(
                query[:, span], keys[slot, :, span], values[slot, :, span], mask, numer, denom, head
            )

    attend(req)
    text_copies.wait_recv()
    done.append(text_copies)
    scale = row_scale(text_squares, width)
    for r in range(requests):
        raw = kept(text[r, 0].astype(F32), keep)
        text_keys[r] = (raw * scale[:, r : r + 1] * gains[3:4, :]).astype(BF)

    def visit(offset, carry):
        for c in chunks:
            value_copy(c, offset).wait_recv()
            key_copy(c, offset).wait_recv()
        attend(lax.rem(req + blocks - offset, blocks))
        return carry

    lax.fori_loop(1, blocks, visit, 0)

    fetches.self_out.wait()
    mixes = [per[c].mix for c in chunks]

    def project(c, weight, part):
        flat = mixes[c][...].reshape(parts * sizes[c], cols)
        part[...] = dot(flat, weight[...]).astype(BF).reshape(part.shape)

    scatters = []
    for c in chunks:
        finish(numer, denom, mixes[c], keep, key_starts[c])
        project(c, ref.v_self_out, per[c].part_self)
        scatters.append(
            Scatter(per[c].part_self, per[c].landed_self, ref.rs_self_send, ref.rs_self_recv, c)
        )

    rows_cross = [per[c].rows_cross for c in chunks]
    hidden, gathers = [], []
    for item in scatters:
        item.relay()
    for c in chunks:
        delta = scatters[c].total()
        hidden_one = states[spans[c], :] + mod_rows(mod, request[c], 2) * delta
        ref.hidden[spans[c], :] = hidden_one
        rows_cross[c][tp] = (layer_norm(hidden_one) * ref.cross_gain[...]).astype(BF)
        gathers.append(Gather(rows_cross[c], ref.cg_send, ref.cg_recv, c, True))
        done += [scatters[c], gathers[c]]
    numer[...] = jnp.zeros_like(numer)
    denom[...] = jnp.zeros_like(denom)
    fetches.cross_query.wait()
    fetches.cross_out.wait()
    slots = text.shape[2]
    text_place = lax.broadcasted_iota(jnp.int32, (1, slots), 1)
    scatters = []
    for c in chunks:
        gathers[c].wait_recv()
        count = parts * sizes[c]
        raw_q = kept(dot(rows_cross[c][...].reshape(count, width), ref.v_cross_query[...]), keep)
        squares = per[c].squares_cross
        squares[tp] = columns_to_rows([square_sums(raw_q)])
        copies = Gather(squares, ref.cs_send, ref.cs_recv, c)
        done.append(copies)
        for earlier in scatters:
            earlier.relay()
        for later in gathers[c + 1 :]:
            later.relay()
        copies.wait_recv()
        scale = row_scale(squares, width)
        cross_q = (raw_q * scale[:, 0:1] * gains[2:3, :]).astype(BF)
        query_request = request_at(
            req * block_rows
            + placed(lax.broadcasted_iota(jnp.int32, (count, 1), 0), segments[c]),
            ends,
        )
        for r in range(requests):
            mask = text_place < jnp.where(query_request == r, lens[0, r], 0)
            for head in range(heads):
                span = slice(head * HD, (head + 1) * HD)
                add_keys(
                    cross_q[:, span],
                    text_keys[r, :, span],
                    text[r, 1, :, span],
                    mask,
                    numer,
                    denom,
                    head,
                    key_starts[c],
                )
        finish(numer, denom, mixes[c], keep, key_starts[c])
        project(c, ref.v_cross_out, per[c].part_cross)
        scatters.append(
            Scatter(per[c].part_cross, per[c].landed_cross, ref.rs_cross_send, ref.rs_cross_recv, c)
        )

    rows_ffn = [per[c].rows_ffn for c in chunks]
    gathers = []
    for item in scatters:
        item.relay()
    for c in chunks:
        delta = scatters[c].total()
        hidden_two = ref.hidden[spans[c], :] + delta
        ref.hidden[spans[c], :] = hidden_two
        rows_ffn[c][core, tp] = (
            layer_norm(hidden_two) * (1.0 + mod_rows(mod, request[c], 4))
            + mod_rows(mod, request[c], 3)
        ).astype(BF)
        gathers.append(Gather(rows_ffn[c].at[core], ref.fg_send, ref.fg_recv, c, True))
        done += [scatters[c], gathers[c]]

    def forward(c, offset):
        view = rows_ffn[c].at[core, lax.rem(tp + parts - offset, parts)]
        copy = remote(view, view, ref.fw_send.at[c, offset], ref.fw_recv.at[c, offset], mate)
        copy.start()
        return copy

    forwards = [[forward(c, 0)] for c in chunks]

    def forward_rest(c):
        gathers[c].relay()
        for offset in gathers[c].copies:
            gathers[c].wait_one(offset)
            forwards[c].append(forward(c, offset))

    fetches.ffn_in.wait()
    fetches.ffn_out.wait()
    scatters = []
    forward_rest(0)
    for c in chunks:
        count = parts * sizes[c]
        acc, half, from_core = per[c].acc, per[c].half, per[c].from_core
        for copy in forwards[c]:
            copy.wait_recv()
        full = rows_ffn[c][...].reshape(2 * count, width)
        acc[...] = jnp.zeros_like(acc)

        def step(i, carry, full=full, acc=acc, count=count):
            span = pl.ds(pl.multiple_of(i * chunk_units, 16), chunk_units)
            up = dot_t(full, ref.v_ffn_in[span, :])
            act = jax.nn.gelu(up, approximate=True).astype(BF)
            acc[...] = acc[...] + dot(act, ref.v_ffn_out[span, :]).reshape(2, count, width)
            return carry

        loops = ref.v_ffn_in.shape[0] // chunk_units
        pause = min(2, loops)
        lax.fori_loop(0, pause, step, 0)
        for earlier in scatters:
            earlier.relay()
        for later in gathers[c + 1 :]:
            later.relay()
        lax.fori_loop(pause, loops, step, 0)
        half[...] = acc[1 - core].astype(BF)
        across = remote(half, from_core, ref.core_send.at[c], ref.core_recv.at[c], mate)
        across.start()
        if c + 1 < len(sizes):
            forward_rest(c + 1)
        across.wait_recv()

        total = acc[core] + from_core[...].astype(F32)
        per[c].part_ffn[...] = total.astype(BF).reshape(per[c].part_ffn.shape)
        scatters.append(
            Scatter(per[c].part_ffn, per[c].landed_ffn, ref.rs_ffn_send, ref.rs_ffn_recv, c)
        )
        done += forwards[c] + [across, scatters[c]]

    speed = ref.speed
    for item in scatters:
        item.relay()
    for c in chunks:
        delta = scatters[c].total()
        last = ref.hidden[spans[c], :] + mod_rows(mod, request[c], 5) * delta
        speed[0, spans[c], :] = dot_t(layer_norm(last).astype(BF), ref.head[...])
    swap = remote(speed.at[0], speed.at[1], ref.swap_send, ref.swap_recv, mate)
    swap.start()
    swap.wait_recv()
    done.append(swap)
    own, other = speed[0], speed[1]
    request = request_at(row_first + lax.broadcasted_iota(jnp.int32, (rows, 1), 0), ends)
    cond = jnp.where(core == 0, own, other)
    plain = jnp.where(core == 0, other, own)
    guided = plain + guide_scale * (cond - plain)
    lane = lax.broadcasted_iota(jnp.int32, (8, HD), 1)
    line = lax.broadcasted_iota(jnp.int32, (8, HD), 0)
    pack = jnp.zeros((8, HD), F32)
    per_row = [
        jnp.sum(cond * cond, axis=1, keepdims=True),
        jnp.sum(guided * guided, axis=1, keepdims=True),
        jnp.max(jnp.abs(guided), axis=1, keepdims=True),
    ]
    for r in range(requests):
        for i, column in enumerate(per_row):
            chosen = jnp.where(request == r, column, 0.0)
            if i < 2:
                value = jnp.sum(chosen, axis=0, keepdims=True)
            else:
                value = jnp.max(chosen, axis=0, keepdims=True)
            pack = jnp.where((lane == r) & (line == i), value, pack)

    def combine(buffer):
        total, top = buffer[0], buffer[0]
        for i in range(1, buffer.shape[0]):
            total = total + buffer[i]
            top = jnp.maximum(top, buffer[i])
        return jnp.where(line == 2, top, total)

    stats_tp, stats_req = ref.stats_tp, ref.stats_req
    stats_tp[tp] = pack
    stat_copies = [Gather(stats_tp, ref.st_send, ref.st_recv, 0)]
    stat_copies[0].wait_recv()
    stats_req[req] = combine(stats_tp)
    for offset in range(1, blocks):
        copy = remote(
            stats_req.at[req],
            stats_req.at[req],
            ref.sr_send.at[offset],
            ref.sr_recv.at[offset],
            {"req": peer_at("req", offset)},
        )
        copy.start()
        stat_copies.append(copy)
    for copy in stat_copies[1:]:
        copy.wait_recv()
    stats = combine(stats_req)
    lanes = lane[:1]
    count = jnp.ones((1, HD), F32)
    step_value = jnp.zeros((1, HD), F32)
    for r in range(requests):
        count = jnp.where(lanes == r, (counts[r] * guided.shape[1]).astype(F32), count)
        step_value = jnp.where(lanes == r, steps[r].astype(F32), step_value)
    cond_rms = jnp.sqrt(stats[0:1] / count + stat_eps)
    guided_rms = jnp.sqrt(stats[1:2] / count + stat_eps)
    factor = rescale_mix * cond_rms / guided_rms + (1.0 - rescale_mix)
    delta_t = noise_level(step_value + 1.0) - noise_level(step_value)
    ref.peak[...] = factor * stats[2:3]
    row_factor = pick(request, [factor[:, r : r + 1] for r in range(requests)])
    row_step = pick(request, [delta_t[:, r : r + 1] for r in range(requests)])
    velocity = row_factor * guided
    moved = ref.latent[...] + row_step * velocity
    new_latent, velocity_out = ref.new_latent, ref.velocity
    own_cols = velocity_out.shape[1]
    velocity_out[...] = jnp.where(core == 0, velocity[:, :own_cols], velocity[:, own_cols:])
    new_latent[...] = jnp.where(core == 0, moved[:, :own_cols], moved[:, own_cols:])
    for copy in done + stat_copies:
        copy.wait_send()

    def drain(offset, carry):
        for c in chunks:
            key_copy(c, offset).wait_send()
            value_copy(c, offset).wait_send()
        return carry

    lax.fori_loop(1, blocks, drain, 0)


def shards(
    latent,
    states,
    token_counts,
    text_lens,
    steps_index,
    modulation,
    self_qkv,
    self_out,
    qk_gains,
    cross_query,
    cross_out,
    cross_gain,
    text_kv,
    ffn_in_weight,
    ffn_out_weight,
    head_weight,
):
    rows = latent.shape[0]
    width = head_weight.shape[0]
    cols = self_out.shape[0]
    heads = cols // HD
    parts, blocks = lax.axis_size("tp"), lax.axis_size("req")
    block_rows = rows * parts
    requests, slots = text_kv.shape[1], text_kv.shape[3]
    units = ffn_in_weight.shape[0]
    chunk_units = units // 5 if units % 80 == 0 else units
    first = -(-rows // 32) * 16
    sizes = (first, rows - first)
    V, S, H = pltpu.VMEM, pltpu.SMEM, pl.ANY
    operands = dict(
        counts=(S, token_counts),
        lens=(S, text_lens),
        steps=(S, steps_index),
        mod=(V, modulation),
        states=(V, states[0]),
        gains=(V, qk_gains),
        cross_gain=(V, cross_gain.reshape(1, width)),
        head=(V, jnp.transpose(head_weight)),
        latent=(V, latent),
        qkv=(H, jnp.transpose(self_qkv, (1, 0, 2))),
        text=(H, text_kv[0]),
        self_out=(H, self_out),
        cross_query=(H, cross_query),
        cross_out=(H, cross_out),
        ffn_in=(H, ffn_in_weight),
        ffn_out=(H, ffn_out_weight),
    )
    small = jax.ShapeDtypeStruct((rows, latent.shape[1] // lax.axis_size("cfg")), F32)
    results = dict(new_latent=small, velocity=small, peak=jax.ShapeDtypeStruct((1, HD), F32))

    def sem(*shape):
        return pltpu.SemaphoreType.DMA(shape) if shape else pltpu.SemaphoreType.DMA

    two = len(sizes)
    by_tp, by_req = sem(two, parts), sem(two, blocks)
    scratch = dict(
        v_qkv=V((3, width, cols), BF),
        v_text=V(text_kv.shape[1:], BF),
        v_self_out=V(self_out.shape, BF),
        v_cross_query=V(cross_query.shape, BF),
        v_cross_out=V(cross_out.shape, BF),
        v_ffn_in=V(ffn_in_weight.shape, BF),
        v_ffn_out=V(ffn_out_weight.shape, BF),
        fetch_sem=sem(7),
        keys=V((blocks, block_rows, cols), BF),
        values=V((blocks, block_rows, cols), BF),
        query=V((block_rows, cols), BF),
        raw_q=V((block_rows, cols), F32),
        raw_k=V((block_rows, cols), F32),
        numer=V((block_rows, cols), F32),
        denom=V((heads, block_rows, HD), F32),
        text_squares=V((parts, 8, slots), F32),
        text_keys=V((requests, slots, cols), BF),
        hidden=V((rows, width), F32),
        speed=V((2, rows, latent.shape[1]), F32),
        stats_tp=V((parts, 8, HD), F32),
        stats_req=V((blocks, 8, HD), F32),
        ag_send=by_tp, ag_recv=by_tp,
        sq_send=by_tp, sq_recv=by_tp,
        tx_send=by_tp, tx_recv=by_tp,
        k_send=by_req, k_recv=by_req,
        v_send=by_req, v_recv=by_req,
        rs_self_send=by_tp, rs_self_recv=by_tp,
        cg_send=by_tp, cg_recv=by_tp,
        cs_send=by_tp, cs_recv=by_tp,
        rs_cross_send=by_tp, rs_cross_recv=by_tp,
        fg_send=by_tp, fg_recv=by_tp,
        fw_send=by_tp, fw_recv=by_tp,
        core_send=sem(two), core_recv=sem(two),
        rs_ffn_send=by_tp, rs_ffn_recv=by_tp,
        swap_send=sem(), swap_recv=sem(),
        st_send=by_tp, st_recv=by_tp,
        sr_send=sem(blocks), sr_recv=sem(blocks),
    )

    def chunk_scratch(size):
        count = parts * size
        wide = V((parts, size, width), BF)
        return dict(
            rows_self=wide, rows_cross=wide, rows_ffn=V((2, parts, size, width), BF),
            part_self=wide, landed_self=wide,
            part_cross=wide, landed_cross=wide,
            part_ffn=wide, landed_ffn=wide,
            squares_self=V((parts, 8, count), F32),
            squares_cross=V((parts, 8, count), F32),
            mix=V((parts, size, cols), BF),
            acc=V((2, count, width), F32),
            half=V((count, width), BF),
            from_core=V((count, width), BF),
        )

    chunk_dicts = [chunk_scratch(size) for size in sizes]
    names = tuple(operands) + tuple(results) + tuple(scratch)
    shapes = list(scratch.values()) + [v for d in chunk_dicts for v in d.values()]
    new_latent, velocity, peak = pl.pallas_call(
        functools.partial(block_kernel, sizes, chunk_units, names, tuple(chunk_dicts[0])),
        out_shape=tuple(results.values()),
        in_specs=[pl.BlockSpec(memory_space=space) for space, _ in operands.values()],
        out_specs=tuple(pl.BlockSpec(memory_space=V) for _ in results),
        scratch_shapes=shapes,
        compiler_params=pltpu.CompilerParams(
            collective_id=0, has_side_effects=True, vmem_limit_bytes=VMEM_LIMIT
        ),
        cost_estimate=pl.CostEstimate(
            flops=16 * block_rows * width * units, bytes_accessed=20 << 20, transcendentals=0
        ),
    )(*[value for _, value in operands.values()])
    return new_latent, velocity, peak[0, :requests]


def solution(mesh):
    in_specs = (
        P(("req", "tp"), None),
        P("cfg", ("req", "tp"), None),
        P(),
        P("cfg", None),
        P(),
        P(),
        P(None, None, "tp"),
        P("tp", None),
        P(None, "tp"),
        P(None, "tp"),
        P("tp", None),
        P(),
        P("cfg", None, None, None, "tp"),
        P(("cfg", "tp"), None),
        P(("cfg", "tp"), None),
        P(),
    )
    out_specs = (P(("req", "tp"), "cfg"), P(("req", "tp"), "cfg"), P())
    return jax.shard_map(shards, mesh=mesh, in_specs=in_specs, out_specs=out_specs, check_vma=False)
```

time: 258 us -> 192 us (0.74)
  Pallas kernels: 238 us -> 184 us
  local copies, waits for them, and re-layouts: 18.4 us -> 6.88 us
    pallas_call x3 -> x1, Pallas kernels: 238 us -> 184 us  [shards(): pl.pallas_call(functools.partial(block_kernel, sizes, chunk_units, names,...]
    unnamed x35 -> x3, local copies, waits for them, and re-layouts: 13.4 us -> 4.42 us
    reshape x1 -> x0, local copies, waits for them, and re-layouts: 4.39 us -> none  [shards(): self_qkv.reshape(width, 3 * cols)]
where the time goes in v2:
time: 192 us; the launch traced here: 191 us
  Pallas kernels  184 us (96%)
  local copies, waits for them, and re-layouts  6.88 us (4%)
    pallas_call x1, Pallas kernels, shards(): pl.pallas_call(functools.partial(block_kernel, sizes, chunk_units, names,...  184 us
    unnamed x3, local copies, waits for them, and re-layouts  4.42 us

profile of v2, /device:TPU:0, one launch (start us, length us, event | category | flops | bytes accessed | tf_op | source)
XLA Modules:
  0.0 191.3 jit_solution(15935535494907972612)
XLA Ops:
  0.6 1.3 reshape.9.refs_6_
  1.9 1.5 copy.19.refs_8_
  3.4 183.8 %shard_map.175 = (f32[96,32]{1,0:T(8,128)}, f32[96,32]{1,0:T(8,128)}, f32[1,128]{1,0:T(1,128)}) custom-call(s32[3]{0:T(128)} %refs_0_.1, s32[1,3]{1,0:T(1,128)} %refs_1_.1, s32[3]{0:T(128)} %refs_2_.1, f32[3,6,1536]{2,1,0:T(8,128)} %refs_3_.1, f32[96,1536]{1,0:T(8,128)} %bitcast.8, f32[4,384]{1,0:T(4,128)} %refs_5_.1, f32[1,1536]{1,0:T(1,128)} %reshape.9.refs_6_, ...), custom_call_target="tpu_custom_call" | custom-call | flops 10569646080 | bytes 20971520 | tf_op jit(solution)/shard_map/pallas_call | solution.py:817
  187.2 1.5 copy.20
  188.6 1.2 slice_bitcast_fusion
  189.8 1.5 copy.21

commit v3 on v2

--- a/solution.py
+++ b/solution.py
@@ -282,7 +282,11 @@
     scores = dot_t(query, key) * HD ** (-0.5)
     weights = jnp.where(mask, jnp.exp(scores), 0.0)
     lanes = denom[head, rows, :]
-    for start in range(0, weights.shape[1], HD):
+    rest = weights.shape[1] % HD
+    if rest:
+        empty = jnp.zeros((weights.shape[0], HD - rest), F32)
+        lanes = lanes + jnp.concatenate([weights[:, weights.shape[1] - rest :], empty], axis=1)
+    for start in range(0, weights.shape[1] - rest, HD):
         lanes = lanes + weights[:, start : start + HD]
     denom[head, rows, :] = lanes
     numer[rows, cols] = numer[rows, cols] + dot(weights.astype(BF), value)
@@ -414,25 +418,24 @@
         key_span = slice(key_starts[c], key_starts[c] + parts * sizes[c])
         values[req, key_span, :] = dot(full, qkv[2]).astype(BF)
         start_all(value_copy, c)
-        for later in gathers[c + 1 :]:
-            later.relay()
         raw_k = kept(dot(full, qkv[1]), keep)
         raw_q = kept(dot(full, qkv[0]), keep)
-        ref.raw_k[key_span, :] = raw_k
-        ref.raw_q[key_span, :] = raw_q
         squares = per[c].squares_self
         squares[tp] = columns_to_rows([square_sums(raw_q), square_sums(raw_k)])
         square_copies.append(Gather(squares, ref.sq_send, ref.sq_recv, c))
-    for c in chunks:
+        for later in gathers[c + 1 :]:
+            later.relay()
         square_copies[c].wait_recv()
-        key_span = slice(key_starts[c], key_starts[c] + parts * sizes[c])
-        scale = row_scale(per[c].squares_self, width)
-        keys[req, key_span, :] = (ref.raw_k[key_span, :] * scale[:, 1:2] * gains[1:2, :]).astype(BF)
+        scale = row_scale(squares, width)
+        keys[req, key_span, :] = (raw_k * scale[:, 1:2] * gains[1:2, :]).astype(BF)
         start_all(key_copy, c)
-        query[key_span, :] = (ref.raw_q[key_span, :] * scale[:, 0:1] * gains[0:1, :]).astype(BF)
+        query[key_span, :] = (raw_q * scale[:, 0:1] * gains[0:1, :]).astype(BF)
     done += gathers + square_copies
 
-    key_place = placed(lax.broadcasted_iota(jnp.int32, (1, block_rows), 1), all_segments)
+    key_places = [
+        placed(lax.broadcasted_iota(jnp.int32, (1, parts * sizes[c]), 1), segments[c])
+        for c in chunks
+    ]
     query_request = request_at(
         req * block_rows
         + placed(lax.broadcasted_iota(jnp.int32, (block_rows, 1), 0), all_segments),
@@ -441,16 +444,24 @@
     lows = pick(query_request, [jnp.int32(0)] + ends[:-1])
     highs = pick(query_request, ends)
 
-    def attend(slot):
-        place = slot * block_rows + key_place
+    def attend(slot, c):
+        place = slot * block_rows + key_places[c]
+        key_span = slice(key_starts[c], key_starts[c] + parts * sizes[c])
         mask = (place >= lows) & (place < highs)
         for head in range(heads):
             span = slice(head * HD, (head + 1) * HD)
             add_keys(
-                query[:, span], keys[slot, :, span], values[slot, :, span], mask, numer, denom, head
+                query[:, span],
+                keys[slot, key_span, span],
+                values[slot, key_span, span],
+                mask,
+                numer,
+                denom,
+                head,
             )
 
-    attend(req)
+    for c in chunks:
+        attend(req, c)
     text_copies.wait_recv()
     done.append(text_copies)
     scale = row_scale(text_squares, width)
@@ -458,14 +469,15 @@
         raw = kept(text[r, 0].astype(F32), keep)
         text_keys[r] = (raw * scale[:, r : r + 1] * gains[3:4, :]).astype(BF)
 
-    def visit(offset, carry):
-        for c in chunks:
+    for c in chunks:
+
+        def visit(offset, carry, c=c):
             value_copy(c, offset).wait_recv()
             key_copy(c, offset).wait_recv()
-        attend(lax.rem(req + blocks - offset, blocks))
-        return carry
-
-    lax.fori_loop(1, blocks, visit, 0)
+            attend(lax.rem(req + blocks - offset, blocks), c)
+            return carry
+
+        lax.fori_loop(1, blocks, visit, 0)
 
     fetches.self_out.wait()
     mixes = [per[c].mix for c in chunks]
@@ -490,7 +502,7 @@
         delta = scatters[c].total()
         hidden_one = states[spans[c], :] + mod_rows(mod, request[c], 2) * delta
         ref.hidden[spans[c], :] = hidden_one
-        rows_cross[c][tp] = (layer_norm(hidden_one) * ref.cross_gain[...]).astype(BF)
+        rows_cross[c][tp] = (layer_norm(hidden_one) * ref.cross_gain[...].reshape(1, width)).astype(BF)
         gathers.append(Gather(rows_cross[c], ref.cg_send, ref.cg_recv, c, True))
         done += [scatters[c], gathers[c]]
     numer[...] = jnp.zeros_like(numer)
@@ -616,13 +628,14 @@
     for c in chunks:
         delta = scatters[c].total()
         last = ref.hidden[spans[c], :] + mod_rows(mod, request[c], 5) * delta
-        speed[0, spans[c], :] = dot_t(layer_norm(last).astype(BF), ref.head[...])
+        ref.final[spans[c], :] = layer_norm(last).astype(BF)
+    speed[0] = dot_t(ref.head[...], ref.final[...])
     swap = remote(speed.at[0], speed.at[1], ref.swap_send, ref.swap_recv, mate)
     swap.start()
     swap.wait_recv()
     done.append(swap)
     own, other = speed[0], speed[1]
-    request = request_at(row_first + lax.broadcasted_iota(jnp.int32, (rows, 1), 0), ends)
+    request = request_at(row_first + lax.broadcasted_iota(jnp.int32, (1, rows), 1), ends)
     cond = jnp.where(core == 0, own, other)
     plain = jnp.where(core == 0, other, own)
     guided = plain + guide_scale * (cond - plain)
@@ -630,17 +643,17 @@
     line = lax.broadcasted_iota(jnp.int32, (8, HD), 0)
     pack = jnp.zeros((8, HD), F32)
     per_row = [
-        jnp.sum(cond * cond, axis=1, keepdims=True),
-        jnp.sum(guided * guided, axis=1, keepdims=True),
-        jnp.max(jnp.abs(guided), axis=1, keepdims=True),
+        jnp.sum(cond * cond, axis=0, keepdims=True),
+        jnp.sum(guided * guided, axis=0, keepdims=True),
+        jnp.max(jnp.abs(guided), axis=0, keepdims=True),
     ]
     for r in range(requests):
         for i, column in enumerate(per_row):
             chosen = jnp.where(request == r, column, 0.0)
             if i < 2:
-                value = jnp.sum(chosen, axis=0, keepdims=True)
+                value = jnp.sum(chosen, axis=1, keepdims=True)
             else:
-                value = jnp.max(chosen, axis=0, keepdims=True)
+                value = jnp.max(chosen, axis=1, keepdims=True)
             pack = jnp.where((lane == r) & (line == i), value, pack)
 
     def combine(buffer):
@@ -672,7 +685,7 @@
     count = jnp.ones((1, HD), F32)
     step_value = jnp.zeros((1, HD), F32)
     for r in range(requests):
-        count = jnp.where(lanes == r, (counts[r] * guided.shape[1]).astype(F32), count)
+        count = jnp.where(lanes == r, (counts[r] * guided.shape[0]).astype(F32), count)
         step_value = jnp.where(lanes == r, steps[r].astype(F32), step_value)
     cond_rms = jnp.sqrt(stats[0:1] / count + stat_eps)
     guided_rms = jnp.sqrt(stats[1:2] / count + stat_eps)
@@ -684,9 +697,9 @@
     velocity = row_factor * guided
     moved = ref.latent[...] + row_step * velocity
     new_latent, velocity_out = ref.new_latent, ref.velocity
-    own_cols = velocity_out.shape[1]
-    velocity_out[...] = jnp.where(core == 0, velocity[:, :own_cols], velocity[:, own_cols:])
-    new_latent[...] = jnp.where(core == 0, moved[:, :own_cols], moved[:, own_cols:])
+    own_cols = velocity_out.shape[0]
+    velocity_out[...] = jnp.where(core == 0, velocity[:own_cols], velocity[own_cols:])
+    new_latent[...] = jnp.where(core == 0, moved[:own_cols], moved[own_cols:])
     for copy in done + stat_copies:
         copy.wait_send()
 
@@ -736,9 +749,9 @@
         mod=(V, modulation),
         states=(V, states[0]),
         gains=(V, qk_gains),
-        cross_gain=(V, cross_gain.reshape(1, width)),
+        cross_gain=(V, cross_gain),
         head=(V, jnp.transpose(head_weight)),
-        latent=(V, latent),
+        latent=(V, jnp.transpose(latent)),
         qkv=(H, jnp.transpose(self_qkv, (1, 0, 2))),
         text=(H, text_kv[0]),
         self_out=(H, self_out),
@@ -747,7 +760,7 @@
         ffn_in=(H, ffn_in_weight),
         ffn_out=(H, ffn_out_weight),
     )
-    small = jax.ShapeDtypeStruct((rows, latent.shape[1] // lax.axis_size("cfg")), F32)
+    small = jax.ShapeDtypeStruct((latent.shape[1] // lax.axis_size("cfg"), rows), F32)
     results = dict(new_latent=small, velocity=small, peak=jax.ShapeDtypeStruct((1, HD), F32))
 
     def sem(*shape):
@@ -767,14 +780,13 @@
         keys=V((blocks, block_rows, cols), BF),
         values=V((blocks, block_rows, cols), BF),
         query=V((block_rows, cols), BF),
-        raw_q=V((block_rows, cols), F32),
-        raw_k=V((block_rows, cols), F32),
         numer=V((block_rows, cols), F32),
         denom=V((heads, block_rows, HD), F32),
         text_squares=V((parts, 8, slots), F32),
         text_keys=V((requests, slots, cols), BF),
         hidden=V((rows, width), F32),
-        speed=V((2, rows, latent.shape[1]), F32),
+        speed=V((2, latent.shape[1], rows), F32),
+        final=V((rows, width), BF),
         stats_tp=V((parts, 8, HD), F32),
         stats_req=V((blocks, 8, HD), F32),
         ag_send=by_tp, ag_recv=by_tp,
@@ -827,7 +839,7 @@
             flops=16 * block_rows * width * units, bytes_accessed=20 << 20, transcendentals=0
         ),
     )(*[value for _, value in operands.values()])
-    return new_latent, velocity, peak[0, :requests]
+    return jnp.transpose(new_latent), jnp.transpose(velocity), peak[0, :requests]
 
 
 def solution(mesh):

time: 192 us -> 187 us (0.974)
  local copies, waits for them, and re-layouts: 6.88 us -> 3.82 us
  Pallas kernels: 184 us -> 182 us
    unnamed x3 -> x2, local copies, waits for them, and re-layouts: 4.42 us -> 2.65 us
where the time goes in v3:
time: 187 us
  Pallas kernels  182 us (97%)
  local copies, waits for them, and re-layouts  3.82 us (2%)
    pallas_call x1, Pallas kernels, shards(): pl.pallas_call(functools.partial(block_kernel, sizes, chunk_units, names,...  182 us

profile of v3, /device:TPU:0, one launch (start us, length us, event | category | flops | bytes accessed | tf_op | source)
XLA Modules:
  0.0 186.7 jit_solution(4736307257350993675)
XLA Ops:
  0.6 182.2 %shard_map.175 = (f32[32,96]{1,0:T(8,128)}, f32[32,96]{1,0:T(8,128)}, f32[1,128]{1,0:T(1,128)}) custom-call(s32[3]{0:T(128)} %refs_0_.1, s32[1,3]{1,0:T(1,128)} %refs_1_.1, s32[3]{0:T(128)} %refs_2_.1, f32[3,6,1536]{2,1,0:T(8,128)} %refs_3_.1, f32[96,1536]{1,0:T(8,128)} %bitcast.13, f32[4,384]{1,0:T(4,128)} %refs_5_.1, f32[1536]{0:T(1024)} %refs_6_.1, ...), custom_call_target="tpu_custom_call" | custom-call | flops 10569646080 | bytes 20971520 | tf_op jit(solution)/shard_map/pallas_call | solution.py:829
  182.8 1.2 slice_bitcast_fusion
  184.0 1.3 copy.21
  185.3 1.3 copy.22
